TPU v7x, 256 devices: a whole 4x4x8 slice. The times are simulated.
256 devices in a mesh: row: 4 (over x), col: 4 (over y), dp: 16 (over z, core).
Axes of the slice: x: 4, y: 4, z: 8, core: 2. Of those that a mesh axis runs over, the one named last changes fastest.
Arguments:
- tokens_in: bfloat16 [3072, 4096], P(('col', 'dp'), 'row'), may hold values from -6 to 6
- out_grad: bfloat16 [3072, 4096], P(('col', 'dp'), 'row'), may hold values from -1.5 to 1.5
- gate_weight: bfloat16 [4096, 14336], P('row', 'col'), may hold values from -0.125 to 0.125
- up_weight: bfloat16 [4096, 14336], P('row', 'col'), may hold values from -0.125 to 0.125
- down_weight: bfloat16 [14336, 4096], P('col', 'row'), may hold values from -0.0625 to 0.0625
- inner_mask: int32 [32, 112], P('row', 'col'), may hold values from 0 to 1, as said below
- outer_mask: int32 [112, 32], P('col', 'row'), may hold values from 0 to 1, as said below
Outputs:
- layer_out: bfloat16 [3072, 4096], P(('col', 'dp'), 'row')
- input_grad: bfloat16 [3072, 4096], P(('col', 'dp'), 'row')
- gate_grad: bfloat16 [4096, 14336], P('row', ('col', 'dp'))
- up_grad: bfloat16 [4096, 14336], P('row', ('col', 'dp'))
- down_grad: bfloat16 [14336, 4096], P(('col', 'dp'), 'row')
Inputs may be any that keep to these rules, and one draw needn't show every extreme that they name: `inner_mask`: 1 keeps a 128 x 128 block of the gate and up projections, 0 drops it; the share of kept blocks differs from one device's tile to another, and a device's tile may keep all of its blocks. `outer_mask`: 1 keeps a 128 x 128 block of the down projection, 0 drops it; the share of kept blocks differs from one device's tile to another, and a device's tile may keep all of its blocks.
All inputs are finite; a program needn't handle non-finite values.
Results may differ from a plain program's by a relative error of at most 0.035.
Values may be sent and summed in bfloat16 or wider, within the bound.
A program may use at most 192 MiB of HBM per device.

v0:
```python
import jax
import jax.numpy as jnp
from jax import lax
from jax.sharding import PartitionSpec as P


def expand_blocks(blocked, edge):
    count_rows, count_cols = blocked.shape
    scaled = blocked.astype(jnp.bfloat16)
    widened = jnp.broadcast_to(scaled[:, None, :, None], (count_rows, edge, count_cols, edge))
    return widened.reshape(count_rows * edge, count_cols * edge)


def contract_last(left, right):
    return lax.dot_general(
        left, right, (((1,), (1,)), ((), ())), preferred_element_type=jnp.float32
    )


def contract_first(left, right):
    return lax.dot_general(
        left, right, (((0,), (0,)), ((), ())), preferred_element_type=jnp.float32
    )


def gated_grads(gate_vals, up_vals, hidden_grad):
    sig = jax.nn.sigmoid(gate_vals)
    gate_back = (hidden_grad * up_vals * sig * (1.0 + gate_vals * (1.0 - sig))).astype(jnp.bfloat16)
    up_back = (hidden_grad * gate_vals * sig).astype(jnp.bfloat16)
    return (gate_back, up_back)


def on_device(tokens_in, out_grad, gate_weight, up_weight, down_weight, inner_mask, outer_mask):
    edge = gate_weight.shape[0] // inner_mask.shape[0]
    inner_full = expand_blocks(inner_mask, edge)
    outer_full = expand_blocks(outer_mask, edge)
    gate_eff = gate_weight * inner_full
    up_eff = up_weight * inner_full
    down_eff = down_weight * outer_full
    width = gate_weight.shape[1]
    joined = jnp.concatenate([gate_eff, up_eff], axis=1)
    inputs_all, grads_all = (
        lax.all_gather(tokens_in, "col", axis=0, tiled=True),
        lax.all_gather(out_grad, "col", axis=0, tiled=True),
    )
    rows_here = inputs_all
    summed = lax.psum_scatter(
        jnp.dot(rows_here, joined, preferred_element_type=jnp.float32).astype(jnp.bfloat16),
        "row",
        scatter_dimension=0,
        tiled=True,
    ).astype(jnp.float32)
    gate_vals = summed[:, :width]
    up_vals = summed[:, width:]
    hidden_share = (jax.nn.silu(gate_vals) * up_vals).astype(jnp.bfloat16)
    hidden = lax.all_gather(hidden_share, "row", axis=0, tiled=True)
    out_part = jnp.dot(hidden, down_eff, preferred_element_type=jnp.float32)
    rows_here = grads_all
    hidden_grad = lax.psum_scatter(
        contract_last(rows_here, down_eff).astype(jnp.bfloat16),
        "row",
        scatter_dimension=0,
        tiled=True,
    ).astype(jnp.float32)
    gate_share, up_share = gated_grads(gate_vals, up_vals, hidden_grad)
    gate_back, up_back = (
        lax.all_gather(gate_share, "row", axis=0, tiled=True),
        lax.all_gather(up_share, "row", axis=0, tiled=True),
    )
    layer_out = lax.psum_scatter(
        out_part.astype(jnp.bfloat16), "col", scatter_dimension=0, tiled=True
    )
    input_part = contract_last(gate_back, gate_eff) + contract_last(up_back, up_eff)
    input_grad = lax.psum_scatter(
        input_part.astype(jnp.bfloat16), "col", scatter_dimension=0, tiled=True
    )
    piece = width // lax.axis_size("dp")
    offset = lax.axis_index("dp") * piece
    inner_slice = lax.dynamic_slice_in_dim(inner_full, offset, piece, 1).astype(jnp.float32)
    outer_slice = lax.dynamic_slice_in_dim(outer_full, offset, piece, 0).astype(jnp.float32)
    gate_part = contract_first(inputs_all, gate_back)
    up_part = contract_first(inputs_all, up_back)
    down_part = contract_first(hidden, grads_all)
    gate_sum, up_sum, down_sum = (
        lax.psum_scatter(
            gate_part.astype(jnp.bfloat16), "dp", scatter_dimension=1, tiled=True
        ).astype(jnp.float32),
        lax.psum_scatter(
            up_part.astype(jnp.bfloat16), "dp", scatter_dimension=1, tiled=True
        ).astype(jnp.float32),
        lax.psum_scatter(
            down_part.astype(jnp.bfloat16), "dp", scatter_dimension=0, tiled=True
        ).astype(jnp.float32),
    )
    gate_grad = (gate_sum * inner_slice).astype(jnp.bfloat16)
    up_grad = (up_sum * inner_slice).astype(jnp.bfloat16)
    down_grad = (down_sum * outer_slice).astype(jnp.bfloat16)
    return (layer_out, input_grad, gate_grad, up_grad, down_grad)


def solution(mesh):
    placed = (
        P(("col", "dp"), "row"),
        P(("col", "dp"), "row"),
        P("row", "col"),
        P("row", "col"),
        P("col", "row"),
        P("row", "col"),
        P("col", "row"),
    )
    return jax.shard_map(
        on_device,
        mesh=mesh,
        in_specs=placed,
        out_specs=(
            P(("col", "dp"), "row"),
            P(("col", "dp"), "row"),
            P("row", ("col", "dp")),
            P("row", ("col", "dp")),
            P(("col", "dp"), "row"),
        ),
        check_vma=False,
    )
```

profile of v0, /device:TPU:2, one launch (start us, length us, event | category | flops | bytes accessed | tf_op | source)
XLA Modules:
  0.0 498.3 jit_solution(13651690926642077578)
XLA Ops:
  7.2 13.3 %all_gather.15 = bf16[192,1024]{1,0:T(8,128)(2,1)S(1)} all-gather(bf16[48,1024]{1,0:T(8,128)(2,1)} %param.7), channel_id=1, replica_groups=mesh['row'=4,'col'=4,'dp'=16] {'col'}, dimensions={0}, use_global_device_ids=true | all-gather | bytes 491520 | tf_op jit(solution)/shard_map/all_gather | solution.py:43
  20.5 10.4 %copy.13 = bf16[1024,3584]{0,1:T(8,128)(2,1)} copy(bf16[1024,3584]{1,0:T(8,128)(2,1)} %param.9) | data formatting | bytes 14680064 | tf_op args[2]
  31.0 10.4 %copy.14 = bf16[1024,3584]{0,1:T(8,128)(2,1)} copy(bf16[1024,3584]{1,0:T(8,128)(2,1)} %param.10) | data formatting | bytes 14680064 | tf_op args[3]
  47.1 6.9 %fusion.29 = (bf16[1024,3584]{0,1:T(8,128)(2,1)}, bf16[1024,3584]{0,1:T(8,128)(2,1)S(1)}) fusion(bf16[1024,3584]{0,1:T(8,128)(2,1)S(1)} %copy-done.2, bf16[448,8,8,128]{3,2,1,0:T(8,128)(2,1)S(1)} %bitcast.43, bf16[1024,3584]{0,1:T(8,128)(2,1)} %copy.14), kind=kLoop, calls=%fused_computation.37 | loop fusion | flops 7340032 | bytes 36700160 | tf_op jit(solution)/shard_map/mul | solution.py:37
  57.0 9.6 %fusion.7 = bf16[192,7168]{1,0:T(8,128)(2,1)} fusion(bf16[192,1024]{1,0:T(8,128)(2,1)S(1)} %all_gather.15, bf16[1024,3584]{0,1:T(8,128)(2,1)S(1)} %get-tuple-element.8, bf16[1024,3584]{0,1:T(8,128)(2,1)} %get-tuple-element.7), kind=kOutput, calls=%fused_computation.5 | convolution fusion | flops 2849308672 | bytes 17825792 | tf_op jit(solution)/shard_map/dot_general | solution.py:48
  66.8 12.5 %all_gather.17 = bf16[192,1024]{1,0:T(8,128)(2,1)S(1)} all-gather(bf16[48,1024]{1,0:T(8,128)(2,1)S(1)} %copy-done.7), channel_id=1, replica_groups=mesh['row'=4,'col'=4,'dp'=16] {'col'}, dimensions={0}, use_global_device_ids=true | all-gather | bytes 491520 | tf_op jit(solution)/shard_map/all_gather | solution.py:44
  83.3 6.8 %fusion.12 = bf16[192,3584]{1,0:T(8,128)(2,1)} fusion(bf16[192,1024]{1,0:T(8,128)(2,1)S(1)} %all_gather.17, bf16[3584,1024]{1,0:T(8,128)(2,1)} %param.11, bf16[448,8,8,128]{3,2,1,0:T(8,128)(2,1)S(1)} %bitcast.45), kind=kOutput, calls=%fused_computation.14 | convolution fusion | flops 1413644288 | bytes 16449536 | tf_op jit(solution)/shard_map/dot_general | solution.py:15
  90.2 15.5 %reduce-scatter.8.cloned.1.call-done = bf16[48,7168]{1,0:T(8,128)(2,1)} async-done(((bf16[192,7168]{1,0:T(8,128)(2,1)}), bf16[48,7168]{1,0:T(8,128)(2,1)}) %reduce-scatter.8.cloned.1.call-update) | async-done | bytes 688144 | tf_op jit(solution)/shard_map/reduce_scatter | solution.py:47
  106.9 28.1 %reduce-scatter.12.cloned.1.call-done = bf16[48,3584]{1,0:T(8,128)(2,1)} async-done(((bf16[192,3584]{1,0:T(8,128)(2,1)}), bf16[48,3584]{1,0:T(8,128)(2,1)}) %reduce-scatter.12.cloned.1.call-update) | async-done | bytes 344080 | tf_op jit(solution)/shard_map/reduce_scatter | solution.py:59
  138.7 27.1 %all-gather.4.cloned.1.call-done = bf16[192,3584]{1,0:T(8,128)(2,1)} async-done(((bf16[48,3584]{1,0:T(8,128)(2,1)}), bf16[192,3584]{1,0:T(8,128)(2,1)}) %all-gather.4.cloned.1.call-update) | async-done | bytes 1376272 | tf_op jit(solution)/shard_map/all_gather | solution.py:56
  165.8 6.5 %convolution_convert_fusion = bf16[3584,1024]{1,0:T(8,128)(2,1)} fusion(bf16[192,3584]{1,0:T(8,128)(2,1)} %all-gather.4.cloned.1.call-done, bf16[192,1024]{1,0:T(8,128)(2,1)S(1)} %all_gather.17), kind=kOutput, calls=%fused_computation.6 | convolution fusion | flops 1412956160 | bytes 9109504 | tf_op jit(solution)/shard_map/dot_general | solution.py:21
  172.3 24.2 %all-gather.8.cloned.1.call-done = bf16[192,3584]{1,0:T(8,128)(2,1)} async-done(((bf16[48,3584]{1,0:T(8,128)(2,1)}), bf16[192,3584]{1,0:T(8,128)(2,1)}) %all-gather.8.cloned.1.call-update) | async-done | bytes 1376272 | tf_op jit(solution)/shard_map/all_gather | solution.py:68
  196.5 6.4 %fusion.11 = bf16[1024,3584]{0,1:T(8,128)(2,1)} fusion(bf16[192,3584]{1,0:T(8,128)(2,1)} %all-gather.8.cloned.1.call-done, bf16[192,1024]{1,0:T(8,128)(2,1)S(1)} %all_gather.15), kind=kOutput, calls=%fused_computation.12 | convolution fusion | flops 1412956160 | bytes 9109504 | tf_op jit(solution)/shard_map/dot_general | solution.py:21
  203.0 24.2 %all-gather.6.cloned.1.call-done = bf16[192,3584]{1,0:T(8,128)(2,1)} async-done(((bf16[48,3584]{1,0:T(8,128)(2,1)}), bf16[192,3584]{1,0:T(8,128)(2,1)}) %all-gather.6.cloned.1.call-update) | async-done | bytes 1376272 | tf_op jit(solution)/shard_map/all_gather | solution.py:67
  227.2 6.4 %fusion.10 = bf16[1024,3584]{0,1:T(8,128)(2,1)} fusion(bf16[192,3584]{1,0:T(8,128)(2,1)} %all-gather.6.cloned.1.call-done, bf16[192,1024]{1,0:T(8,128)(2,1)S(1)} %all_gather.15), kind=kOutput, calls=%fused_computation.11 | convolution fusion | flops 1412956160 | bytes 9109504 | tf_op jit(solution)/shard_map/dot_general | solution.py:21
  233.7 7.6 %fusion.17 = bf16[192,1024]{1,0:T(8,128)(2,1)} fusion(bf16[192,3584]{1,0:T(8,128)(2,1)S(1)} %copy-done.5, bf16[3584,1024]{1,0:T(8,128)(2,1)} %param.11, bf16[448,8,8,128]{3,2,1,0:T(8,128)(2,1)} %bitcast.46), kind=kOutput, calls=%fused_computation.20 | convolution fusion | flops 1413152768 | bytes 16449536 | tf_op jit(solution)/shard_map/dot_general | solution.py:57
  246.8 5.6 %fusion.16 = bf16[192,1024]{1,0:T(8,128)(2,1)} fusion(f32[192,1024]{1,0:T(8,128)S(1)} %fusion.30, bf16[192,3584]{1,0:T(8,128)(2,1)S(1)} %copy-done.4, bf16[1024,3584]{0,1:T(8,128)(2,1)} %copy-done.3), kind=kOutput, calls=%fused_computation.19 | convolution fusion | flops 1409679360 | bytes 9895936 | tf_op jit(solution)/shard_map/dot_general | solution.py:15
  252.4 7.9 %copy.31 = bf16[448,8,8,128]{3,1,2,0:T(8,128)(2,1)} copy(bf16[448,8,8,128]{3,2,1,0:T(8,128)(2,1)} %bitcast.44) | data formatting | bytes 14680064
  260.3 8.0 %copy.30 = bf16[448,8,8,128]{3,1,2,0:T(8,128)(2,1)} copy(bf16[448,8,8,128]{3,2,1,0:T(8,128)(2,1)} %bitcast.47) | data formatting | bytes 14680064
  268.3 31.5 %reduce-scatter.20.cloned.1.call-done = bf16[224,1024]{1,0:T(8,128)(2,1)} async-done(((bf16[3584,1024]{1,0:T(8,128)(2,1)}), bf16[224,1024]{1,0:T(8,128)(2,1)}) %reduce-scatter.20.cloned.1.call-update) | async-done | bytes 458768 | tf_op jit(solution)/shard_map/reduce_scatter | solution.py:91
  302.0 67.9 %reduce-scatter.18.cloned.1.call-done = bf16[1024,224]{0,1:T(8,128)(2,1)} async-done(((bf16[1024,3584]{0,1:T(8,128)(2,1)}), bf16[1024,224]{0,1:T(8,128)(2,1)}) %reduce-scatter.18.cloned.1.call-update) | async-done | bytes 458768 | tf_op jit(solution)/shard_map/reduce_scatter | solution.py:88
  369.9 70.1 %reduce-scatter.16.cloned.1.call-done = bf16[1024,224]{0,1:T(8,128)(2,1)} async-done(((bf16[1024,3584]{0,1:T(8,128)(2,1)}), bf16[1024,224]{0,1:T(8,128)(2,1)}) %reduce-scatter.16.cloned.1.call-update) | async-done | bytes 458768 | tf_op jit(solution)/shard_map/reduce_scatter | solution.py:85
  442.5 22.8 %reduce-scatter.10.cloned.1.call-done = bf16[48,1024]{1,0:T(8,128)(2,1)} async-done(((bf16[192,1024]{1,0:T(8,128)(2,1)}), bf16[48,1024]{1,0:T(8,128)(2,1)}) %reduce-scatter.10.cloned.1.call-update) | async-done | bytes 98320 | tf_op jit(solution)/shard_map/reduce_scatter | solution.py:70
  465.3 26.2 %reduce-scatter.14.cloned.1.call-done = bf16[48,1024]{1,0:T(8,128)(2,1)} async-done(((bf16[192,1024]{1,0:T(8,128)(2,1)}), bf16[48,1024]{1,0:T(8,128)(2,1)}) %reduce-scatter.14.cloned.1.call-update) | async-done | bytes 98320 | tf_op jit(solution)/shard_map/reduce_scatter | solution.py:74
  (51 shorter events, 28.1 us)
Async XLA Ops:
  7.2 98.5 %reduce-scatter.8.cloned.1.call-start = ((), (), s32[]{:S(2)}) async-start(), calls=%async_computation.7 | async-start | bytes 3440640 | tf_op jit(solution)/shard_map/reduce_scatter | solution.py:47
  20.5 10.4 %copy-start.8 = (s32[8,28]{1,0:T(8,128)S(1)}, s32[8,28]{1,0:T(8,128)}, u32[]{:S(2)}) copy-start(s32[8,28]{1,0:T(8,128)} %param.12) | copy-start | bytes 2692
  41.4 5.7 %copy-start.2 = (bf16[1024,3584]{0,1:T(8,128)(2,1)S(1)}, bf16[1024,3584]{0,1:T(8,128)(2,1)}, u32[]{:S(2)}) copy-start(bf16[1024,3584]{0,1:T(8,128)(2,1)} %copy.13) | copy-start | bytes 22020100
  42.4 11.6 %copy-start = (bf16[8,128,28,128]{1,0,3,2:T(8,128)(2,1)}, bf16[8,128,28,128]{1,0,3,2:T(8,128)(2,1)S(1)}, u32[]{:S(2)}) copy-start(bf16[8,128,28,128]{1,0,3,2:T(8,128)(2,1)S(1)} %broadcast_in_dim.4) | copy-start | bytes 22020100
  54.0 2.9 copy-start.3
  57.0 9.7 %copy-start.9 = (s32[28,8]{0,1:T(8,128)S(1)}, s32[28,8]{0,1:T(8,128)}, u32[]{:S(2)}) copy-start(s32[28,8]{0,1:T(8,128)} %param.13) | copy-start | bytes 2692
  57.0 9.8 %copy-start.7 = (bf16[48,1024]{1,0:T(8,128)(2,1)S(1)}, bf16[48,1024]{1,0:T(8,128)(2,1)}, u32[]{:S(2)}) copy-start(bf16[48,1024]{1,0:T(8,128)(2,1)} %param.8) | copy-start | bytes 294916
  66.6 68.4 %reduce-scatter.12.cloned.1.call-start = ((), (), s32[]{:S(2)}) async-start(), calls=%async_computation.10 | async-start | bytes 1720320 | tf_op jit(solution)/shard_map/reduce_scatter | solution.py:59
  80.3 3.0 copy-start.1
  90.2 75.6 %all-gather.4.cloned.1.call-start = ((), (), s32[]{:S(2)}) async-start(), calls=%async_computation.8 | async-start | bytes 1720320 | tf_op jit(solution)/shard_map/all_gather | solution.py:56
  137.3 59.2 %all-gather.8.cloned.1.call-start = ((), (), s32[]{:S(2)}) async-start(), calls=%async_computation.12 | async-start | bytes 1720320 | tf_op jit(solution)/shard_map/all_gather | solution.py:68
  137.9 89.3 %all-gather.6.cloned.1.call-start = ((), (), s32[]{:S(2)}) async-start(), calls=%async_computation.11 | async-start | bytes 1720320 | tf_op jit(solution)/shard_map/all_gather | solution.py:67
  138.5 161.4 %reduce-scatter.20.cloned.1.call-start = ((), (), s32[]{:S(2)}) async-start(), calls=%async_computation.16 | async-start | bytes 7798784 | tf_op jit(solution)/shard_map/reduce_scatter | solution.py:91
  172.3 197.6 %reduce-scatter.18.cloned.1.call-start = ((), (), s32[]{:S(2)}) async-start(), calls=%async_computation.15 | async-start | bytes 7798784 | tf_op jit(solution)/shard_map/reduce_scatter | solution.py:88
  202.9 30.8 %copy-start.5 = (bf16[192,3584]{1,0:T(8,128)(2,1)S(1)}, bf16[192,3584]{1,0:T(8,128)(2,1)}, u32[]{:S(2)}) copy-start(bf16[192,3584]{1,0:T(8,128)(2,1)} %all-gather.4.cloned.1.call-done) | copy-start | bytes 4128772
  202.9 237.1 %reduce-scatter.16.cloned.1.call-start = ((), (), s32[]{:S(2)}) async-start(), calls=%async_computation.14 | async-start | bytes 7798784 | tf_op jit(solution)/shard_map/reduce_scatter | solution.py:85
  233.7 8.0 %copy-start.6 = (bf16[192,3584]{1,0:T(8,128)(2,1)S(1)}, bf16[192,3584]{1,0:T(8,128)(2,1)}, u32[]{:S(2)}) copy-start(bf16[192,3584]{1,0:T(8,128)(2,1)} %all-gather.6.cloned.1.call-done) | copy-start | bytes 4128772
  233.7 231.6 %reduce-scatter.10.cloned.1.call-start = ((), (), s32[]{:S(2)}) async-start(), calls=%async_computation.9 | async-start | bytes 491520 | tf_op jit(solution)/shard_map/reduce_scatter | solution.py:70
  241.4 5.4 %copy-start.4 = (bf16[192,3584]{1,0:T(8,128)(2,1)S(1)}, bf16[192,3584]{1,0:T(8,128)(2,1)}, u32[]{:S(2)}) copy-start(bf16[192,3584]{1,0:T(8,128)(2,1)} %all-gather.8.cloned.1.call-done) | copy-start | bytes 4128772
  241.4 250.1 %reduce-scatter.14.cloned.1.call-start = ((), (), s32[]{:S(2)}) async-start(), calls=%async_computation.13 | async-start | bytes 491520 | tf_op jit(solution)/shard_map/reduce_scatter | solution.py:74
Sparse Core Ops, SparseCore 0:
  66.7 38.9 reduce-scatter.7
  108.3 26.7 reduce-scatter.11
  137.5 28.2 all-gather.3
  168.2 28.2 all-gather.7
  198.9 28.2 all-gather.5
  229.8 70.0 reduce-scatter.19
  302.6 67.2 reduce-scatter.17
  372.6 67.3 reduce-scatter.15
  443.3 21.9 reduce-scatter.9
  468.3 23.1 reduce-scatter.13
where the time goes:
time: 499 us; the launch traced here: 498 us
  waiting for transfers between devices  339 us (68%)
  matrix products  54 us (11%)
  local copies, waits for them, and re-layouts  49.7 us (10%)
  blocking collectives  25.8 us (5%)
  other arithmetic  14.9 us (3%)
  between operations  14.3 us (3%)
    reduce_scatter x1, waiting for transfers between devices, on_device(): lax.psum_scatter(gate_part.astype(jnp.bfloat16), 'dp', scatter_dimension=...  70.1 us
    reduce_scatter x1, waiting for transfers between devices, on_device(): lax.psum_scatter(up_part.astype(jnp.bfloat16), 'dp', scatter_dimension=1,...  67.9 us
    unnamed x24, local copies, waits for them, and re-layouts  47.5 us
    reduce_scatter x1, waiting for transfers between devices, on_device(): lax.psum_scatter(down_part.astype(jnp.bfloat16), 'dp', scatter_dimension=...  31.5 us
    reduce_scatter x1, waiting for transfers between devices, on_device(): lax.psum_scatter(contract_last(rows_here, down_eff).astype(jnp.bfloat16),...  28.1 us
    all_gather x1, waiting for transfers between devices, on_device(): hidden = lax.all_gather(hidden_share, 'row', axis=0, tiled=True)  27.1 us
    reduce_scatter x1, waiting for transfers between devices, on_device(): lax.psum_scatter(input_part.astype(jnp.bfloat16), 'col', scatter_dimensio...  26.2 us
    all_gather x1, waiting for transfers between devices, on_device(): lax.all_gather(gate_share, 'row', axis=0, tiled=True)  24.2 us
  transfers between devices with their start and end apart: 10, of which 10 were waited for; matrix products, arithmetic and copies ran while one was open for 14% of the time, Pallas kernels for 0%

commit v1 on v0

v1 whole, which is shorter than its diff:
```python
import jax
import jax.numpy as jnp
from jax import lax
from jax.sharding import PartitionSpec as P


def expand_blocks(blocked, edge):
    count_rows, count_cols = blocked.shape
    scaled = blocked.astype(jnp.bfloat16)
    widened = jnp.broadcast_to(scaled[:, None, :, None], (count_rows, edge, count_cols, edge))
    return widened.reshape(count_rows * edge, count_cols * edge)


def contract_last(left, right):
    return lax.dot_general(
        left, right, (((1,), (1,)), ((), ())), preferred_element_type=jnp.float32
    )


def contract_first(left, right):
    return lax.dot_general(
        left, right, (((0,), (0,)), ((), ())), preferred_element_type=jnp.float32
    )


def gated_grads(gate_vals, up_vals, hidden_grad):
    sig = jax.nn.sigmoid(gate_vals)
    gate_back = (hidden_grad * up_vals * sig * (1.0 + gate_vals * (1.0 - sig))).astype(jnp.bfloat16)
    up_back = (hidden_grad * gate_vals * sig).astype(jnp.bfloat16)
    return (gate_back, up_back)


def scatter_tokens(part):
    over_col = lax.psum_scatter(
        part.astype(jnp.bfloat16), "col", scatter_dimension=0, tiled=True
    )
    return lax.psum_scatter(over_col, "dp", scatter_dimension=0, tiled=True)


def on_device(tokens_in, out_grad, gate_weight, up_weight, down_weight, inner_mask, outer_mask):
    edge = gate_weight.shape[0] // inner_mask.shape[0]
    piece = gate_weight.shape[1] // lax.axis_size("dp")
    offset = lax.axis_index("dp") * piece
    inner_slice = lax.dynamic_slice_in_dim(expand_blocks(inner_mask, edge), offset, piece, 1)
    outer_slice = lax.dynamic_slice_in_dim(expand_blocks(outer_mask, edge), offset, piece, 0)
    gate_eff = lax.dynamic_slice_in_dim(gate_weight, offset, piece, 1) * inner_slice
    up_eff = lax.dynamic_slice_in_dim(up_weight, offset, piece, 1) * inner_slice
    down_eff = lax.dynamic_slice_in_dim(down_weight, offset, piece, 0) * outer_slice
    joined = jnp.concatenate([gate_eff, up_eff], axis=1)
    inputs_all = lax.all_gather(tokens_in, ("col", "dp"), axis=0, tiled=True)
    grads_all = lax.all_gather(out_grad, ("col", "dp"), axis=0, tiled=True)
    parts = jnp.concatenate(
        [
            jnp.dot(inputs_all, joined, preferred_element_type=jnp.float32),
            contract_last(grads_all, down_eff),
        ],
        axis=1,
    ).astype(jnp.bfloat16)
    summed = lax.psum_scatter(parts, "row", scatter_dimension=0, tiled=True).astype(jnp.float32)
    gate_vals = summed[:, :piece]
    up_vals = summed[:, piece : 2 * piece]
    hidden_grad = summed[:, 2 * piece :]
    hidden_share = (jax.nn.silu(gate_vals) * up_vals).astype(jnp.bfloat16)
    gate_share, up_share = gated_grads(gate_vals, up_vals, hidden_grad)
    shares = jnp.concatenate([gate_share, up_share, hidden_share], axis=1)
    whole = lax.all_gather(shares, "row", axis=0, tiled=True)
    backs = whole[:, : 2 * piece]
    hidden = whole[:, 2 * piece :]
    layer_out = scatter_tokens(jnp.dot(hidden, down_eff, preferred_element_type=jnp.float32))
    input_grad = scatter_tokens(contract_last(backs, joined))
    back_grads = contract_first(inputs_all, backs)
    inner_scale = inner_slice.astype(jnp.float32)
    gate_grad = (back_grads[:, :piece] * inner_scale).astype(jnp.bfloat16)
    up_grad = (back_grads[:, piece:] * inner_scale).astype(jnp.bfloat16)
    down_grad = (contract_first(hidden, grads_all) * outer_slice.astype(jnp.float32)).astype(
        jnp.bfloat16
    )
    return (layer_out, input_grad, gate_grad, up_grad, down_grad)


def solution(mesh):
    placed = (
        P(("col", "dp"), "row"),
        P(("col", "dp"), "row"),
        P("row", "col"),
        P("row", "col"),
        P("col", "row"),
        P("row", "col"),
        P("col", "row"),
    )
    return jax.shard_map(
        on_device,
        mesh=mesh,
        in_specs=placed,
        out_specs=(
            P(("col", "dp"), "row"),
            P(("col", "dp"), "row"),
            P("row", ("col", "dp")),
            P("row", ("col", "dp")),
            P(("col", "dp"), "row"),
        ),
        check_vma=False,
    )
```

time: 499 us -> 553 us (1.11)
  waiting for transfers between devices: 339 us -> 480 us
  local copies, waits for them, and re-layouts: 49.7 us -> 14.3 us
  blocking collectives: 25.8 us -> 0 us
  matrix products: 54 us -> 33.9 us
    all_gather x3, waiting for transfers between devices: 75.5 us -> 195 us  [the longest x1 74.5 us: on_device(): grads_all = lax.all_gather(out_grad, ('col', 'dp'), axis=0, tiled=True)]
    unnamed x24 -> x16, local copies, waits for them, and re-layouts: 47.5 us -> 10.2 us
    all_gather x2 -> x0, blocking collectives: 25.8 us -> none  [the longest x1 13.3 us: on_device(): lax.all_gather(tokens_in, 'col', axis=0, tiled=True)]
    reduce_scatter x7 -> x5, waiting for transfers between devices: 262 us -> 284 us  [the longest x2 130 us: scatter_tokens(): lax.psum_scatter(part.astype(jnp.bfloat16), 'col', scatter_dimension=0, t...]
    dot_general x3 -> x2, matrix products: 19.3 us -> 9.49 us  [contract_first(): lax.dot_general(left, right, (((0,), (0,)), ((), ())), preferred_element_...]
    dot_general x3 -> x2, matrix products: 17.5 us -> 12.4 us  [contract_last(): lax.dot_general(left, right, (((1,), (1,)), ((), ())), preferred_element_...]
  transfers between devices with their start and end apart: 10 -> 8, of which waited for: 10 -> 8; matrix products, arithmetic and copies ran while one was open for 14% -> 7% of each run, Pallas kernels for 0% -> 0%
where the time goes in v1:
time: 553 us
  waiting for transfers between devices  480 us (87%)
  matrix products  33.9 us (6%)
  local copies, waits for them, and re-layouts  14.3 us (3%)
  between operations  14.3 us (3%)
  other arithmetic  9.44 us (2%)
    reduce_scatter x2, waiting for transfers between devices, scatter_tokens(): lax.psum_scatter(part.astype(jnp.bfloat16), 'col', scatter_dimension=0, t...  130 us
    reduce_scatter x2, waiting for transfers between devices, scatter_tokens(): return lax.psum_scatter(over_col, 'dp', scatter_dimension=0, tiled=True)  109 us
    all_gather x1, waiting for transfers between devices, on_device(): grads_all = lax.all_gather(out_grad, ('col', 'dp'), axis=0, tiled=True)  74.5 us
    all_gather x1, waiting for transfers between devices, on_device(): inputs_all = lax.all_gather(tokens_in, ('col', 'dp'), axis=0, tiled=True)  69.8 us
    all_gather x1, waiting for transfers between devices, on_device(): whole = lax.all_gather(shares, 'row', axis=0, tiled=True)  50.7 us
    reduce_scatter x1, waiting for transfers between devices, on_device(): lax.psum_scatter(parts, 'row', scatter_dimension=0, tiled=True)  44.1 us
    dot_general x2, matrix products, contract_last(): lax.dot_general(left, right, (((1,), (1,)), ((), ())), preferred_element_...  12.4 us
  transfers between devices with their start and end apart: 8, of which 8 were waited for; matrix products, arithmetic and copies ran while one was open for 7% of the time, Pallas kernels for 0%

profile of v1, /device:TPU:2, one launch (start us, length us, event | category | flops | bytes accessed | tf_op | source)
XLA Modules:
  0.0 552.6 jit_solution(14321040934940629037)
XLA Ops:
  8.7 1.8 constant_dynamic-slice_fusion
  11.1 1.0 broadcast_in_dim.4
  12.1 4.9 copy.23
  17.1 1.0 broadcast_in_dim.5
  18.2 4.9 copy.22
  23.0 2.1 dynamic-slice_multiply_fusion.2
  25.1 69.8 %all-gather.4.cloned.1.call-done = bf16[3072,1024]{1,0:T(8,128)(2,1)} async-done(((bf16[48,1024]{1,0:T(8,128)(2,1)}), bf16[3072,1024]{1,0:T(8,128)(2,1)}) %all-gather.4.cloned.1.call-update) | async-done | bytes 6291472 | tf_op jit(solution)/shard_map/all_gather | solution.py:50
  94.9 6.0 %fusion = bf16[3072,448]{0,1:T(8,128)(2,1)S(1)} fusion(bf16[3072,1024]{1,0:T(8,128)(2,1)} %all-gather.4.cloned.1.call-done, bf16[1024,224]{0,1:T(8,128)(2,1)} %get-tuple-element.8, bf16[1024,224]{0,1:T(8,128)(2,1)S(1)} %get-tuple-element.7), kind=kOutput, calls=%fused_computation.6 | convolution fusion | flops 2821783552 | bytes 9961472 | tf_op jit(solution)/shard_map/dot_general | solution.py:54
  100.9 74.5 %all-gather.6.cloned.1.call-done = bf16[3072,1024]{1,0:T(8,128)(2,1)} async-done(((bf16[48,1024]{1,0:T(8,128)(2,1)}), bf16[3072,1024]{1,0:T(8,128)(2,1)}) %all-gather.6.cloned.1.call-update) | async-done | bytes 6291472 | tf_op jit(solution)/shard_map/all_gather | solution.py:51
  175.4 5.1 fusion.1
  180.5 2.3 pad_maximum_fusion
  183.1 44.1 %reduce-scatter.6.cloned.1.call-done = bf16[768,672]{0,1:T(8,128)(2,1)} async-done(((bf16[3072,672]{0,1:T(8,128)(2,1)}), bf16[768,672]{0,1:T(8,128)(2,1)}) %reduce-scatter.6.cloned.1.call-update) | async-done | bytes 1032208 | tf_op jit(solution)/shard_map/reduce_scatter | solution.py:59
  227.1 1.4 convert_element_type.42
  228.9 1.0 pad_maximum_fusion.1
  230.1 50.7 %all-gather.8.cloned.1.call-done = bf16[3072,672]{0,1:T(8,128)(2,1)} async-done(((bf16[768,672]{0,1:T(8,128)(2,1)}), bf16[3072,672]{0,1:T(8,128)(2,1)}) %all-gather.8.cloned.1.call-update) | async-done | bytes 4128784 | tf_op jit(solution)/shard_map/all_gather | solution.py:66
  280.8 7.3 %convolution_convert_fusion = bf16[3072,1024]{1,0:T(8,128)(2,1)} fusion(bf16[3072,672]{0,1:T(8,128)(2,1)} %all-gather.8.cloned.1.call-done, bf16[1024,224]{0,1:T(8,128)(2,1)S(1)} %copy-done.1, bf16[1024,224]{0,1:T(8,128)(2,1)S(1)} %get-tuple-element.7), kind=kOutput, calls=%fused_computation.2 | convolution fusion | flops 2823553024 | bytes 9961472 | tf_op jit(solution)/shard_map/dot_general | solution.py:15
  288.1 6.1 %convolution_convert_fusion.1 = bf16[3072,1024]{1,0:T(8,128)(2,1)} fusion(bf16[3072,672]{0,1:T(8,128)(2,1)} %all-gather.8.cloned.1.call-done, bf16[3584,1024]{1,0:T(8,128)(2,1)} %param.11, s32[]{:T(128)S(6)} %select_n.2, bf16[3584,1024]{1,0:T(8,128)(2,1)} %bitcast.27), kind=kOutput, calls=%fused_computation.3 | convolution fusion | flops 1413349376 | bytes 8585220 | tf_op jit(solution)/shard_map/dot_general | solution.py:69
  294.3 61.5 %reduce-scatter.12.cloned.1.call-done = bf16[768,1024]{1,0:T(8,128)(2,1)} async-done(((bf16[3072,1024]{1,0:T(8,128)(2,1)}), bf16[768,1024]{1,0:T(8,128)(2,1)}) %reduce-scatter.12.cloned.1.call-update) | async-done | bytes 1572880 | tf_op jit(solution)/shard_map/reduce_scatter | solution.py:34
  355.8 68.8 %reduce-scatter.8.cloned.1.call-done = bf16[768,1024]{1,0:T(8,128)(2,1)} async-done(((bf16[3072,1024]{1,0:T(8,128)(2,1)}), bf16[768,1024]{1,0:T(8,128)(2,1)}) %reduce-scatter.8.cloned.1.call-update) | async-done | bytes 1572880 | tf_op jit(solution)/shard_map/reduce_scatter | solution.py:34
  424.7 6.1 %fusion.5 = f32[1024,448]{0,1:T(8,128)S(1)} fusion(bf16[3072,1024]{1,0:T(8,128)(2,1)} %all-gather.4.cloned.1.call-done, bf16[3072,672]{0,1:T(8,128)(2,1)} %all-gather.8.cloned.1.call-done), kind=kOutput, calls=%fused_computation.12 | convolution fusion | flops 2818572288 | bytes 10878976 | tf_op jit(solution)/shard_map/dot_general | solution.py:21
  430.8 2.2 fusion.12
  433.0 3.4 fusion.8
  436.4 49.5 %reduce-scatter.14.cloned.1.call-done = bf16[48,1024]{1,0:T(8,128)(2,1)} async-done(((bf16[768,1024]{1,0:T(8,128)(2,1)}), bf16[48,1024]{1,0:T(8,128)(2,1)}) %reduce-scatter.14.cloned.1.call-update) | async-done | bytes 98320 | tf_op jit(solution)/shard_map/reduce_scatter | solution.py:37
  485.9 59.8 %reduce-scatter.10.cloned.1.call-done = bf16[48,1024]{1,0:T(8,128)(2,1)} async-done(((bf16[768,1024]{1,0:T(8,128)(2,1)}), bf16[48,1024]{1,0:T(8,128)(2,1)}) %reduce-scatter.10.cloned.1.call-update) | async-done | bytes 98320 | tf_op jit(solution)/shard_map/reduce_scatter | solution.py:37
  (36 shorter events, 3.0 us)
Async XLA Ops:
  7.2 3.8 copy-start.2
  7.2 87.7 %all-gather.4.cloned.1.call-start = ((), (), s32[]{:S(2)}) async-start(), calls=%async_computation.5 | async-start | bytes 6389760 | tf_op jit(solution)/shard_map/all_gather | solution.py:50
  7.9 167.5 %all-gather.6.cloned.1.call-start = ((), (), s32[]{:S(2)}) async-start(), calls=%async_computation.6 | async-start | bytes 6389760 | tf_op jit(solution)/shard_map/all_gather | solution.py:51
  8.7 218.5 %reduce-scatter.6.cloned.1.call-start = ((), (), s32[]{:S(2)}) async-start(), calls=%async_computation.7 | async-start | bytes 5160960 | tf_op jit(solution)/shard_map/reduce_scatter | solution.py:59
  12.1 4.9 copy-start.3
  182.8 97.9 %copy-start.1 = (bf16[1024,224]{0,1:T(8,128)(2,1)S(1)}, bf16[1024,224]{0,1:T(8,128)(2,1)}, u32[]{:S(2)}) copy-start(bf16[1024,224]{0,1:T(8,128)(2,1)} %get-tuple-element.8) | copy-start | bytes 1376260
  182.9 97.9 %all-gather.8.cloned.1.call-start = ((), (), s32[]{:S(2)}) async-start(), calls=%async_computation.8 | async-start | bytes 5160960 | tf_op jit(solution)/shard_map/all_gather | solution.py:66
  230.0 125.7 %reduce-scatter.12.cloned.1.call-start = ((), (), s32[]{:S(2)}) async-start(), calls=%async_computation.11 | async-start | bytes 7864320 | tf_op jit(solution)/shard_map/reduce_scatter | solution.py:34
  288.1 136.6 %reduce-scatter.8.cloned.1.call-start = ((), (), s32[]{:S(2)}) async-start(), calls=%async_computation.9 | async-start | bytes 7864320 | tf_op jit(solution)/shard_map/reduce_scatter | solution.py:34
  294.2 191.7 %reduce-scatter.14.cloned.1.call-start = ((), (), s32[]{:S(2)}) async-start(), calls=%async_computation.12 | async-start | bytes 1671168 | tf_op jit(solution)/shard_map/reduce_scatter | solution.py:37
  355.8 190.0 %reduce-scatter.10.cloned.1.call-start = ((), (), s32[]{:S(2)}) async-start(), calls=%async_computation.10 | async-start | bytes 1671168 | tf_op jit(solution)/shard_map/reduce_scatter | solution.py:37
  424.6 8.4 %slice-start = ((s8[6291456]{0:T(1024)(128)(4,1)}), s8[2097152]{0:T(1024)(128)(4,1)S(1)}, s32[]{:S(2)}) async-start(s8[6291456]{0:T(1024)(128)(4,1)} %bitcast.29), calls=%async_computation.13 | async-start | bytes 4194304
  424.6 8.3 %copy-start = (bf16[3072,672]{0,1:T(8,128)(2,1)S(1)}, bf16[3072,672]{0,1:T(8,128)(2,1)}, u32[]{:S(2)}) copy-start(bf16[3072,672]{0,1:T(8,128)(2,1)} %all-gather.8.cloned.1.call-done) | copy-start | bytes 12386308
  424.7 8.3 %slice-start.1 = ((s8[6291456]{0:T(1024)(128)(4,1)}), s8[4194304]{0:T(1024)(128)(4,1)S(1)}, s32[]{:S(2)}) async-start(s8[6291456]{0:T(1024)(128)(4,1)} %bitcast.29), calls=%async_computation.14 | async-start | bytes 8388608
Sparse Core Ops, SparseCore 0:
  10.8 84.0 all-gather.3
  97.6 77.6 all-gather.5
  183.0 44.1 reduce-scatter.5
  230.1 50.5 all-gather.7
  288.2 67.4 reduce-scatter.11
  358.3 66.2 reduce-scatter.7
  427.9 57.9 reduce-scatter.13
  489.0 56.6 reduce-scatter.9

commit v2 on v1

v2 whole, which is shorter than its diff:
```python
import jax
import jax.numpy as jnp
from jax import lax
from jax.experimental import pallas as pl
from jax.experimental.pallas import tpu as pltpu
from jax.sharding import PartitionSpec as P

MESH = pl.DeviceIdType.MESH
F32 = jnp.float32
BF16 = jnp.bfloat16
CHUNKS = 3
ROWS = 16
SLOTS = 8
GROUPS = ((0, 1), (1, 3), (3, 5), (5, 8))


def expand_blocks(blocked, edge):
    count_rows, count_cols = blocked.shape
    scaled = blocked.astype(BF16)
    widened = jnp.broadcast_to(scaled[:, None, :, None], (count_rows, edge, count_cols, edge))
    return widened.reshape(count_rows * edge, count_cols * edge)


def dot(left, right, dims):
    return lax.dot_general(left, right, ((dims[:1], dims[1:]), ((), ())), preferred_element_type=F32)


def layer_kernel(
    tok_ref, grad_ref, wgu_ref, wd_ref, inner_ref, outer_ref,
    lo_ref, ig_ref, gu_ref, dn_ref,
    act, part, opp_in, sum_in, share, outs, ring_in, rows_out, rows_in, acc, pair_out, pair_in,
    send_sem, recv_sem, pair_send, pair_recv,
):
    x = lax.axis_index("row")
    y = lax.axis_index("col")
    d = lax.axis_index("dp")
    z = d // 2
    k = lax.rem(d, 2)
    xr, xl, xo = lax.rem(x + 1, 4), lax.rem(x + 3, 4), lax.rem(x + 2, 4)
    x_right, x_left = (xr, y, d), (xl, y, d)
    y_right = (x, lax.rem(y + 1, 4), d)
    y_left = (x, lax.rem(y + 3, 4), d)
    y_far = (x, lax.rem(y + 2, 4), d)
    z_right = (x, y, lax.rem(z + 1, 8) * 2 + k)
    z_left = (x, y, lax.rem(z + 7, 8) * 2 + k)
    sibling = (x, y, z * 2 + 1 - k)
    unit = wd_ref.shape[0]
    full = part.shape[2]
    half = full // 2
    lo_half, hi_half = pl.ds(0, half), pl.ds(half, half)

    barrier = pltpu.get_barrier_semaphore()
    peers = (x_right, x_left, y_right, y_left, y_far, z_right, z_left, sibling)
    for peer in peers:
        pl.semaphore_signal(barrier, inc=1, device_id=peer, device_id_type=MESH)
    for c in range(CHUNKS):
        act[c, 0, 0, 0] = tok_ref[pl.ds(c * ROWS, ROWS), :]
        act[c, 0, 0, 1] = grad_ref[pl.ds(c * ROWS, ROWS), :]
    pl.semaphore_wait(barrier, len(peers))

    copies = {}

    def add(name, src, dst, peer, land=None):
        copies[name] = (len(copies), src, dst, peer, dst if land is None else land)

    for step in range(4):
        up_from, up_to = (0, 1, 3, 5)[step], (1, 3, 5, 7)[step]
        dn_from, dn_to = (0, 2, 4, 6)[step], (2, 4, 6, 7)[step]
        if step < 3:
            add(f"zp{step}", lambda c, a=up_from: act.at[c, 0, a], lambda c, a=up_to: act.at[c, 0, a], z_right)
            add(f"zm{step}", lambda c, a=dn_from: act.at[c, 0, a], lambda c, a=dn_to: act.at[c, 0, a], z_left)
        else:
            add("zp3", lambda c: act.at[c, 0, 5, 0], lambda c: act.at[c, 0, 7, 0], z_right)
            add("zm3", lambda c: act.at[c, 0, 6, 1], lambda c: act.at[c, 0, 7, 1], z_left)
    for g, (a, b) in enumerate(GROUPS):
        sl = pl.ds(a, b - a)
        add(f"yp{g}", lambda c, sl=sl: act.at[c, 0, sl], lambda c, sl=sl: act.at[c, 1, sl], y_right)
        add(f"ym{g}", lambda c, sl=sl: act.at[c, 0, sl], lambda c, sl=sl: act.at[c, 2, sl], y_left)
        add(f"yfp{g}", lambda c, sl=sl: act.at[c, 1, sl, 0], lambda c, sl=sl: act.at[c, 3, sl, 0], y_right)
        add(f"yfm{g}", lambda c, sl=sl: act.at[c, 2, sl, 1], lambda c, sl=sl: act.at[c, 3, sl, 1], y_left)
    add("xop", lambda c: part.at[c, xo, lo_half], lambda c: opp_in.at[c, 0], x_right)
    add("xom", lambda c: part.at[c, xo, hi_half], lambda c: opp_in.at[c, 1], x_left)
    add("xdp", lambda c: part.at[c, xr, hi_half], lambda c: sum_in.at[c, 0, hi_half], x_right)
    add("xdm", lambda c: part.at[c, xl, lo_half], lambda c: sum_in.at[c, 1, lo_half], x_left)
    add("xsp", lambda c: part.at[c, xr, lo_half], lambda c: sum_in.at[c, 0, lo_half], x_right)
    add("xsm", lambda c: part.at[c, xl, hi_half], lambda c: sum_in.at[c, 1, hi_half], x_left)
    add("xap", lambda c: share.at[c, x], lambda c: share.at[c, x], x_right, lambda c: share.at[c, xl])
    add("xam", lambda c: share.at[c, x], lambda c: share.at[c, x], x_left, lambda c: share.at[c, xr])
    add("xfp", lambda c: share.at[c, xl, lo_half], lambda c: share.at[c, xl, lo_half], x_right,
        lambda c: share.at[c, xo, lo_half])
    add("xfm", lambda c: share.at[c, xr, hi_half], lambda c: share.at[c, xr, hi_half], x_left,
        lambda c: share.at[c, xo, hi_half])
    first, last = pl.ds(0, 4), pl.ds(4, 4)
    add("rp0", lambda c: outs.at[c, 7, first], lambda c: ring_in.at[c, 0, 0, first], z_right)
    add("rm0", lambda c: outs.at[c, 7, last], lambda c: ring_in.at[c, 1, 0, last], z_left)
    for step in range(1, 4):
        a, b = (6, 4, 2)[step - 1], (5, 3, 1)[step - 1]
        add(f"rp{step}", lambda c, a=a: outs.at[c, a], lambda c, step=step: ring_in.at[c, 0, step], z_right)
        add(f"rm{step}", lambda c, b=b: outs.at[c, b], lambda c, step=step: ring_in.at[c, 1, step], z_left)
    add("tp", lambda c: rows_out.at[c, 2], lambda c: rows_in.at[c, 0], y_right)
    add("tm", lambda c: rows_out.at[c, 1], lambda c: rows_in.at[c, 1], y_left)
    add("tf", lambda c: rows_out.at[c, 3], lambda c: rows_in.at[c, 2], y_far)
    assert len(copies) == send_sem.shape[1]

    def describe(src, dst, c, index, peer):
        return pltpu.make_async_remote_copy(
            src_ref=src, dst_ref=dst, send_sem=send_sem.at[c, index], recv_sem=recv_sem.at[c, index],
            device_id=peer, device_id_type=MESH,
        )

    def start(c, *names):
        for name in names:
            index, src, dst, peer, land = copies[name]
            describe(src(c), dst(c), c, index, peer).start()

    def got(c, *names):
        for name in names:
            index, src, dst, peer, land = copies[name]
            describe(land(c), land(c), c, index, peer).wait_recv()

    def sent(c, *names):
        for name in names:
            index, src, dst, peer, land = copies[name]
            describe(src(c), dst(c), c, index, peer).wait_send()

    def gather(step, c):
        if step == 0:
            start(c, "zp0", "zm0", "yp0", "ym0")
        elif step == 1:
            got(c, "zp0", "zm0")
            start(c, "zp1", "zm1", "yp1", "ym1")
            got(c, "yp0", "ym0")
            start(c, "yfp0", "yfm0")
        elif step == 2:
            got(c, "zp1", "zm1")
            start(c, "zp2", "zm2", "yp2", "ym2")
        elif step == 3:
            got(c, "zp2", "zm2")
            start(c, "zp3", "zm3")
            got(c, "yp1", "ym1")
            start(c, "yfp1", "yfm1")
        elif step == 4:
            got(c, "zp3", "zm3")
            start(c, "yp3", "ym3")
            got(c, "yp2", "ym2")
            start(c, "yfp2", "yfm2")
        elif step == 5:
            got(c, "yp3", "ym3")
            start(c, "yfp3", "yfm3")
        else:
            for g in range(len(GROUPS)):
                got(c, f"yfp{g}", f"yfm{g}")

    def rows_of(c, first_y, count, which):
        return act[c, pl.ds(first_y, count), :, which].reshape(count * SLOTS * ROWS, -1)

    def project(c):
        @pl.loop(0, 2)
        def _(h):
            gu = dot(wgu_ref[...], rows_of(c, 2 * h, 2, 0), (1, 1)).astype(BF16)
            part[c, 2 * h, pl.ds(0, 2 * unit)] = gu[:, :128]
            part[c, 2 * h + 1, pl.ds(0, 2 * unit)] = gu[:, 128:]
            hg = dot(wd_ref[...], rows_of(c, 2 * h, 2, 1), (1, 1)).astype(BF16)
            part[c, 2 * h, pl.ds(2 * unit, unit)] = hg[:, :128]
            part[c, 2 * h + 1, pl.ds(2 * unit, unit)] = hg[:, 128:]

        start(c, "xop", "xom", "xdp", "xdm")

    tile = 112

    def middle_sums(c):
        got(c, "xop", "xom")

        @pl.loop(0, half // tile)
        def _(i):
            at = pl.ds(pl.multiple_of(i * tile, 16), tile)
            up = pl.ds(pl.multiple_of(half + i * tile, 16), tile)
            part[c, xr, at] = (part[c, xr, at].astype(F32) + opp_in[c, 0, at].astype(F32)).astype(BF16)
            part[c, xl, up] = (part[c, xl, up].astype(F32) + opp_in[c, 1, at].astype(F32)).astype(BF16)

        start(c, "xsp", "xsm")

    def gated(c):
        got(c, "xdp", "xdm", "xsp", "xsm")

        def total(at):
            return part[c, x, at].astype(F32) + sum_in[c, 0, at].astype(F32) + sum_in[c, 1, at].astype(F32)

        step = 64

        @pl.loop(0, unit // step)
        def _(i):
            at = pl.ds(pl.multiple_of(i * step, 16), step)
            at_up = pl.ds(pl.multiple_of(unit + i * step, 16), step)
            at_dn = pl.ds(pl.multiple_of(2 * unit + i * step, 16), step)
            gate, up, grad = total(at), total(at_up), total(at_dn)
            sig = 1.0 / (1.0 + jnp.exp(-gate))
            act_gate = gate * sig
            share[c, x, at_dn] = (act_gate * up).astype(BF16)
            share[c, x, at] = (grad * up * sig * (1.0 + gate * (1.0 - sig))).astype(BF16)
            share[c, x, at_up] = (grad * act_gate).astype(BF16)

        start(c, "xap", "xam")

    def forward_shares(c):
        got(c, "xap", "xam")
        start(c, "xfp", "xfm")

    def joined(c, rows, first_part, count):
        return jnp.concatenate([share[c, first_part + i, rows] for i in range(count)], axis=1)

    def outputs(c):
        got(c, "xfp", "xfm")

        @pl.loop(0, 2)
        def _(h):
            hidden = joined(c, pl.ds(2 * unit, unit), 2 * h, 2)
            lo = dot(hidden, wd_ref[...], (0, 0)).astype(BF16).reshape(2, SLOTS, ROWS, -1)
            outs[c, :, 2 * h] = lo[0]
            outs[c, :, 2 * h + 1] = lo[1]
            backs = joined(c, pl.ds(0, 2 * unit), 2 * h, 2)
            ig = dot(backs, wgu_ref[...], (0, 0)).astype(BF16).reshape(2, SLOTS, ROWS, -1)
            outs[c, :, 4 + 2 * h] = ig[0]
            outs[c, :, 5 + 2 * h] = ig[1]

        start(c, "rp0", "rm0")

    def ring(step, c):
        got(c, f"rp{step - 1}", f"rm{step - 1}")
        if step < 4:
            a, b = (6, 4, 2)[step - 1], (5, 3, 1)[step - 1]

            def bump(slot, way, i):
                outs[c, slot, i] = (outs[c, slot, i].astype(F32) + ring_in[c, way, step - 1, i].astype(F32)).astype(BF16)

            if step == 1:

                @pl.loop(0, 4)
                def _(i):
                    bump(a, 0, i)
                    bump(b, 1, i + 4)
            else:

                @pl.loop(0, 8)
                def _(i):
                    bump(a, 0, i)
                    bump(b, 1, i)

            start(c, f"rp{step}", f"rm{step}")
        else:
            for dest in range(1, 4):
                for which in range(2):
                    rows_out[c, dest, which] = own_sum(c, which * 4 + dest).astype(BF16)
            start(c, "tp", "tm", "tf")

    def own_sum(c, i):
        return outs[c, 0, i].astype(F32) + ring_in[c, 0, 3, i].astype(F32) + ring_in[c, 1, 3, i].astype(F32)

    def finish_rows(c):
        got(c, "tp", "tm", "tf")
        at = pl.ds(pl.multiple_of(c * ROWS, ROWS), ROWS)
        for which, ref in ((0, lo_ref), (1, ig_ref)):
            total = own_sum(c, which * 4)
            for i in range(3):
                total = total + rows_in[c, i, which].astype(F32)
            ref[at, :] = total.astype(BF16)

    width = 256

    def weight_grads(c):
        @pl.loop(0, acc.shape[1] // width)
        def _(n):
            lanes = pl.ds(pl.multiple_of(n * width, width), width)
            tokens = act[c, :, :, 0, :, lanes].reshape(4 * SLOTS * ROWS, width)
            grads = act[c, :, :, 1, :, lanes].reshape(4 * SLOTS * ROWS, width)
            gu = dot(joined(c, pl.ds(0, 2 * unit), 0, 4), tokens, (1, 0))
            dn = dot(joined(c, pl.ds(2 * unit, unit), 0, 4), grads, (1, 0))
            acc[pl.ds(0, 2 * unit), lanes] += gu
            acc[pl.ds(2 * unit, unit), lanes] += dn

    own = unit // 2

    def pair_copy():
        return pltpu.make_async_remote_copy(
            src_ref=pair_out, dst_ref=pair_in, send_sem=pair_send, recv_sem=pair_recv,
            device_id=sibling, device_id_type=MESH,
        )

    def own_rows(i, which):
        return pl.ds(pl.multiple_of(i * unit + which * own, 32), own)

    def pair_start():
        for i in range(3):
            pair_out[i] = acc[own_rows(i, 1 - k), :].astype(BF16)
        pair_copy().start()

    def pair_finish():
        pair_copy().wait_recv()
        mine = pl.ds(pl.multiple_of(k * own, 32), own)
        for i in range(3):
            total = acc[own_rows(i, k), :] + pair_in[i].astype(F32)
            if i < 2:
                gu_ref[i] = (total * inner_ref[mine, :].astype(F32)).astype(BF16)
            else:
                dn_ref[...] = (total * outer_ref[mine, :].astype(F32)).astype(BF16)

    acc[...] = jnp.zeros_like(acc)

    @pl.loop(0, CHUNKS + 2)
    def _(s):
        ahead, now, behind = s, s - 1, s - 2

        def when_ahead(f, *a):
            pl.when(ahead < CHUNKS)(lambda: f(*a, ahead))

        def when_now(f, *a):
            pl.when((now >= 0) & (now < CHUNKS))(lambda: f(*a, now))

        def when_behind(f, *a):
            pl.when(behind >= 0)(lambda: f(*a, behind))

        def at_end(f):
            pl.when(s == CHUNKS + 1)(f)

        when_ahead(gather, 0)
        when_now(project)
        when_behind(ring, 1)
        when_ahead(gather, 1)
        when_behind(weight_grads)
        at_end(pair_start)
        when_now(middle_sums)
        when_behind(ring, 2)
        when_ahead(gather, 2)
        when_now(gated)
        when_behind(ring, 3)
        at_end(pair_finish)
        when_ahead(gather, 3)
        when_now(forward_shares)
        when_behind(ring, 4)
        when_ahead(gather, 4)
        when_ahead(gather, 5)
        when_now(outputs)
        when_behind(finish_rows)
        when_ahead(gather, 6)
        pl.when(behind >= 0)(lambda: sent(behind, *copies))

    pair_copy().wait_send()


def on_device(tokens_in, out_grad, gate_weight, up_weight, down_weight, inner_mask, outer_mask):
    edge = gate_weight.shape[0] // inner_mask.shape[0]
    features, width = gate_weight.shape
    chips = lax.axis_size("dp") // 2
    unit = width // chips
    own = unit // 2
    offset = lax.axis_index("dp") // 2 * unit
    inner_slice = lax.dynamic_slice_in_dim(expand_blocks(inner_mask.T, edge), offset, unit, 0)
    outer_slice = lax.dynamic_slice_in_dim(expand_blocks(outer_mask, edge), offset, unit, 0)
    gate_eff = lax.dynamic_slice_in_dim(gate_weight, offset, unit, 1).T * inner_slice
    up_eff = lax.dynamic_slice_in_dim(up_weight, offset, unit, 1).T * inner_slice
    down_eff = lax.dynamic_slice_in_dim(down_weight, offset, unit, 0) * outer_slice
    joined = jnp.concatenate([gate_eff, up_eff], axis=0)
    rows = tokens_in.shape[0]
    full = 3 * unit
    copies = 45
    vmem = pl.BlockSpec(memory_space=pltpu.VMEM)
    layer_out, input_grad, gate_up, down_grad = pl.pallas_call(
        layer_kernel,
        name="layer",
        out_shape=(
            jax.ShapeDtypeStruct((rows, features), BF16),
            jax.ShapeDtypeStruct((rows, features), BF16),
            jax.ShapeDtypeStruct((2, own, features), BF16),
            jax.ShapeDtypeStruct((own, features), BF16),
        ),
        in_specs=[vmem] * 6,
        out_specs=(vmem,) * 4,
        scratch_shapes=[
            pltpu.VMEM((CHUNKS, 4, SLOTS, 2, ROWS, features), BF16),
            pltpu.VMEM((CHUNKS, 4, full, 128), BF16),
            pltpu.VMEM((CHUNKS, 2, full // 2, 128), BF16),
            pltpu.VMEM((CHUNKS, 2, full, 128), BF16),
            pltpu.VMEM((CHUNKS, 4, full, 128), BF16),
            pltpu.VMEM((CHUNKS, SLOTS, 8, ROWS, features), BF16),
            pltpu.VMEM((CHUNKS, 2, 4, 8, ROWS, features), BF16),
            pltpu.VMEM((CHUNKS, 4, 2, ROWS, features), BF16),
            pltpu.VMEM((CHUNKS, 3, 2, ROWS, features), BF16),
            pltpu.VMEM((full, features), F32),
            pltpu.VMEM((3, own, features), BF16),
            pltpu.VMEM((3, own, features), BF16),
            pltpu.SemaphoreType.DMA((CHUNKS, copies)),
            pltpu.SemaphoreType.DMA((CHUNKS, copies)),
            pltpu.SemaphoreType.DMA,
            pltpu.SemaphoreType.DMA,
        ],
        compiler_params=pltpu.CompilerParams(
            collective_id=0, has_side_effects=True, vmem_limit_bytes=58 * 2**20
        ),
    )(tokens_in, out_grad, joined, down_eff, inner_slice, outer_slice)
    return (layer_out, input_grad, gate_up[0].T, gate_up[1].T, down_grad)


def solution(mesh):
    placed = (
        P(("col", "dp"), "row"),
        P(("col", "dp"), "row"),
        P("row", "col"),
        P("row", "col"),
        P("col", "row"),
        P("row", "col"),
        P("col", "row"),
    )
    return jax.shard_map(
        on_device,
        mesh=mesh,
        in_specs=placed,
        out_specs=(
            P(("col", "dp"), "row"),
            P(("col", "dp"), "row"),
            P("row", ("col", "dp")),
            P("row", ("col", "dp")),
            P(("col", "dp"), "row"),
        ),
        check_vma=False,
    )
```

time: 553 us -> 199 us (0.36)
  waiting for transfers between devices: 480 us -> 0 us
  Pallas kernels: 0 us -> 165 us
  matrix products: 33.9 us -> 0 us
  between operations: 14.3 us -> 0.74 us
  local copies, waits for them, and re-layouts: 14.3 us -> 24 us
    reduce_scatter x5 -> x0, waiting for transfers between devices: 284 us -> none  [the longest x2 130 us: scatter_tokens(): lax.psum_scatter(part.astype(jnp.bfloat16), 'col', scatter_dimension=0, t...]
    all_gather x3 -> x0, waiting for transfers between devices: 195 us -> none  [the longest x1 74.5 us: on_device(): grads_all = lax.all_gather(out_grad, ('col', 'dp'), axis=0, tiled=True)]
    pallas_call x0 -> x1, Pallas kernels: none -> 165 us  [on_device(): pl.pallas_call(layer_kernel, name='layer', out_shape=(jax.ShapeDtypeStruc...]
    dot_general x6 -> x0, matrix products: 33.9 us -> none  [the longest x2 12.4 us: contract_last(): lax.dot_general(left, right, (((1,), (1,)), ((), ())), preferred_element_...]
    unnamed x16 -> x13, local copies, waits for them, and re-layouts: 10.2 us -> 15.7 us
  transfers between devices with their start and end apart: 8 -> 0, of which waited for: 8 -> 0; matrix products, arithmetic and copies ran while one was open for 7% -> 0% of each run, Pallas kernels for 0% -> 0%
where the time goes in v2:
time: 199 us; the launch traced here: 197 us
  Pallas kernels  165 us (83%)
  local copies, waits for them, and re-layouts  24 us (12%)
  other arithmetic  6.73 us (3%)
    pallas_call x1, Pallas kernels, on_device(): pl.pallas_call(layer_kernel, name='layer', out_shape=(jax.ShapeDtypeStruc...  165 us
    unnamed x13, local copies, waits for them, and re-layouts  15.7 us

profile of v2, /device:TPU:2, one launch (start us, length us, event | category | flops | bytes accessed | tf_op | source)
XLA Modules:
  0.0 196.6 jit_solution(15781085112013921052)
XLA Ops:
  0.6 0.0 copy-start.1
  0.7 1.8 constant_dynamic-slice_fusion.3
  2.5 0.5 copy.16
  3.0 0.0 copy-done.1
  3.0 0.1 copy.15
  3.1 1.0 broadcast_in_dim.5
  4.1 0.0 copy-start.2
  4.1 4.9 %copy.22 = bf16[448,8,8,128]{3,1,2,0:T(8,128)(2,1)} copy(bf16[448,8,8,128]{3,2,1,0:T(8,128)(2,1)S(1)} %bitcast.24) | data formatting | bytes 14680064
  9.0 0.0 copy-done.2
  9.1 0.1 copy.13
  9.2 1.0 broadcast_in_dim.4
  10.2 4.8 %copy.23 = bf16[448,8,8,128]{3,1,2,0:T(8,128)(2,1)} copy(bf16[448,8,8,128]{3,2,1,0:T(8,128)(2,1)S(1)} %bitcast.25) | data formatting | bytes 14680064
  15.0 4.0 %bitcast_multiply_fusion.1 = (bf16[448,1024]{1,0:T(8,128)(2,1)}, bf16[448,1024]{1,0:T(8,128)(2,1)S(1)}, bf16[448,1024]{1,0:T(8,128)(2,1)}, bf16[448,1024]{1,0:T(8,128)(2,1)}) fusion(bf16[1024,448]{0,1:T(8,128)(2,1)S(1)} %copy.16, bf16[3584,1024]{1,0:T(8,128)(2,1)} %bitcast.27, s32[]{:T(128)S(6)} %select_n.13, bf16[3584,1024]{1,0:T(8,128)(2,1)} %bitcast.26, ...), kind=kLoop, calls=%fused_computation.4 | loop fusion | flops 3670016 | bytes 7340036 | tf_op jit(solution)/shard_map/mul | solution.py:359
  19.0 0.0 copy-start
  19.0 2.1 %constant_dynamic-slice_fusion.1 = bf16[1024,448]{1,0:T(8,128)(2,1)S(1)} fusion(bf16[1024,3584]{1,0:T(8,128)(2,1)} %param.10, s32[]{:T(128)S(6)} %select_n.13), kind=kLoop, calls=%fused_computation.10 | loop fusion | bytes 1835012 | tf_op jit(solution)/shard_map/dynamic_slice | solution.py:360
  21.1 0.5 copy.17
  21.6 0.1 bitcast_multiply_fusion
  21.7 2.6 %pad_maximum_fusion.wgu_ref = bf16[896,1024]{1,0:T(8,128)(2,1)} fusion(bf16[448,1024]{1,0:T(8,128)(2,1)S(1)} %bitcast_multiply_fusion, bf16[448,1024]{1,0:T(8,128)(2,1)} %get-tuple-element.13), kind=kLoop, calls=%fused_computation.2 | loop fusion | flops 3670016 | bytes 3670016 | tf_op jit(solution)/shard_map/concatenate | solution.py:362
  24.4 0.0 copy-done
  24.4 165.2 %layer.1 = (bf16[48,1024]{1,0:T(8,128)(2,1)}, bf16[48,1024]{1,0:T(8,128)(2,1)}, bf16[2,224,1024]{2,1,0:T(8,128)(2,1)}, bf16[224,1024]{1,0:T(8,128)(2,1)}) custom-call(bf16[48,1024]{1,0:T(8,128)(2,1)} %tok_ref.1, bf16[48,1024]{1,0:T(8,128)(2,1)} %grad_ref.1, bf16[896,1024]{1,0:T(8,128)(2,1)} %pad_maximum_fusion.wgu_ref, ...), custom_call_target="tpu_custom_call" | custom-call | tf_op jit(solution)/shard_map/layer/pallas_call | solution.py:367
  189.6 2.1 %slice_bitcast_fusion = (bf16[1024,224]{0,1:T(8,128)(2,1)}, bf16[1024,224]{0,1:T(8,128)(2,1)}) fusion(bf16[2,224,1024]{2,1,0:T(8,128)(2,1)} %get-tuple-element.11), kind=kLoop, calls=%fused_computation.6 | loop fusion | bytes 1835008 | tf_op jit(solution)/shard_map/transpose | solution.py:400
  191.7 1.5 copy.27
  193.3 1.5 copy.28
  194.8 1.8 copy.29
  (2 shorter events, 0.0 us)
Async XLA Ops:
  0.6 2.3 %copy-start.1 = (s32[28,8]{0,1:T(8,128)S(1)}, s32[28,8]{0,1:T(8,128)}, u32[]{:S(2)}) copy-start(s32[28,8]{0,1:T(8,128)} %param.13) | copy-start | bytes 2692
  4.1 4.9 %copy-start.2 = (s32[8,28]{1,0:T(8,128)S(1)}, s32[8,28]{1,0:T(8,128)}, u32[]{:S(2)}) copy-start(s32[8,28]{1,0:T(8,128)} %param.12) | copy-start | bytes 2692
  19.0 5.4 %copy-start = (bf16[448,1024]{1,0:T(8,128)(2,1)}, bf16[448,1024]{1,0:T(8,128)(2,1)S(1)}, u32[]{:S(2)}) copy-start(bf16[448,1024]{1,0:T(8,128)(2,1)S(1)} %get-tuple-element.14.inner_ref) | copy-start | bytes 2752516

commit v3 on v2

v3 whole, which is shorter than its diff:
```python
import jax
import jax.numpy as jnp
from jax import lax
from jax.experimental import pallas as pl
from jax.experimental.pallas import tpu as pltpu
from jax.sharding import PartitionSpec as P

MESH = pl.DeviceIdType.MESH
F32 = jnp.float32
BF16 = jnp.bfloat16
CHUNKS = 3
ROWS = 16
SLOTS = 8
EDGE = 128
GRAIN = 32
WINDOW = 512
GROUPS = ((0, 1), (1, 3), (3, 5), (5, 8))
COPIES = 64


def dot(left, right, dims):
    return lax.dot_general(left, right, ((dims[:1], dims[1:]), ((), ())), preferred_element_type=F32)


def layer_kernel(
    tok_ref, grad_ref, gate_hbm, up_hbm, down_hbm, inner_ref, outer_ref,
    lo_ref, ig_ref, gate_ref, up_ref, down_ref,
    act, part, opp_in, sum_in, share, outs, ring_in, rows_out, rows_in, acc, pair_out, pair_in,
    wgu, wd, window, turned,
    send_sem, recv_sem, pair_send, pair_recv, load_sem,
):
    x = lax.axis_index("row")
    y = lax.axis_index("col")
    d = lax.axis_index("dp")
    z = d // 2
    k = lax.rem(d, 2)
    xr, xl, xo = lax.rem(x + 1, 4), lax.rem(x + 3, 4), lax.rem(x + 2, 4)
    x_right, x_left = (xr, y, d), (xl, y, d)
    y_right = (x, lax.rem(y + 1, 4), d)
    y_left = (x, lax.rem(y + 3, 4), d)
    y_far = (x, lax.rem(y + 2, 4), d)
    z_right = (x, y, lax.rem(z + 1, 8) * 2 + k)
    z_left = (x, y, lax.rem(z + 7, 8) * 2 + k)
    sibling = (x, y, z * 2 + 1 - k)
    own = wd.shape[1]
    unit = 2 * own
    full = part.shape[3]
    half = full // 2
    lo_half, hi_half = pl.ds(0, half), pl.ds(half, half)

    base = pl.multiple_of((7 * z) // 2 * EDGE, EDGE)
    loads = [
        pltpu.make_async_copy(gate_hbm.at[:, pl.ds(base, WINDOW)], window.at[0], load_sem.at[0]),
        pltpu.make_async_copy(up_hbm.at[:, pl.ds(base, WINDOW)], window.at[1], load_sem.at[1]),
    ]
    for h in range(2):
        rows = pl.ds(pl.multiple_of(z * unit + h * own, GRAIN), own)
        loads.append(pltpu.make_async_copy(down_hbm.at[rows, :], wd.at[h], load_sem.at[2 + h]))
    for load in loads:
        load.start()

    barrier = pltpu.get_barrier_semaphore()
    peers = (x_right, x_left, y_right, y_left, y_far, z_right, z_left, sibling)
    for peer in peers:
        pl.semaphore_signal(barrier, inc=1, device_id=peer, device_id_type=MESH)
    for c in range(CHUNKS):
        act[c, 0, 0, 0] = tok_ref[pl.ds(c * ROWS, ROWS), :]
        act[c, 0, 0, 1] = grad_ref[pl.ds(c * ROWS, ROWS), :]
    pl.semaphore_wait(barrier, len(peers))

    copies = {}

    def add(name, src, dst, peer, land=None):
        copies[name] = (len(copies), src, dst, peer, dst if land is None else land)

    for step in range(3):
        up_from, up_to = (0, 1, 3)[step], (1, 3, 5)[step]
        dn_from, dn_to = (0, 2, 4)[step], (2, 4, 6)[step]
        add(f"zp{step}", lambda c, a=up_from: act.at[c, 0, a], lambda c, a=up_to: act.at[c, 0, a], z_right)
        add(f"zm{step}", lambda c, a=dn_from: act.at[c, 0, a], lambda c, a=dn_to: act.at[c, 0, a], z_left)
    add("zp3", lambda c: act.at[c, 0, 5, 0], lambda c: act.at[c, 0, 7, 0], z_right)
    add("zm3", lambda c: act.at[c, 0, 6, 1], lambda c: act.at[c, 0, 7, 1], z_left)
    for g, (a, b) in enumerate(GROUPS):
        sl = pl.ds(a, b - a)
        add(f"yp{g}", lambda c, sl=sl: act.at[c, 0, sl], lambda c, sl=sl: act.at[c, 1, sl], y_right)
        add(f"ym{g}", lambda c, sl=sl: act.at[c, 0, sl], lambda c, sl=sl: act.at[c, 2, sl], y_left)
        add(f"yfp{g}", lambda c, sl=sl: act.at[c, 1, sl, 0], lambda c, sl=sl: act.at[c, 3, sl, 0], y_right)
        add(f"yfm{g}", lambda c, sl=sl: act.at[c, 2, sl, 1], lambda c, sl=sl: act.at[c, 3, sl, 1], y_left)
    for h in range(2):
        add(f"xop{h}", lambda c, h=h: part.at[c, h, xo, lo_half], lambda c, h=h: opp_in.at[c, h, 0], x_right)
        add(f"xom{h}", lambda c, h=h: part.at[c, h, xo, hi_half], lambda c, h=h: opp_in.at[c, h, 1], x_left)
        add(f"xdp{h}", lambda c, h=h: part.at[c, h, xr, hi_half], lambda c, h=h: sum_in.at[c, h, 0, hi_half], x_right)
        add(f"xdm{h}", lambda c, h=h: part.at[c, h, xl, lo_half], lambda c, h=h: sum_in.at[c, h, 1, lo_half], x_left)
        add(f"xsp{h}", lambda c, h=h: part.at[c, h, xr, lo_half], lambda c, h=h: sum_in.at[c, h, 0, lo_half], x_right)
        add(f"xsm{h}", lambda c, h=h: part.at[c, h, xl, hi_half], lambda c, h=h: sum_in.at[c, h, 1, hi_half], x_left)
        add(f"xap{h}", lambda c, h=h: share.at[c, h, x], lambda c, h=h: share.at[c, h, x], x_right,
            lambda c, h=h: share.at[c, h, xl])
        add(f"xam{h}", lambda c, h=h: share.at[c, h, x], lambda c, h=h: share.at[c, h, x], x_left,
            lambda c, h=h: share.at[c, h, xr])
        add(f"xfp{h}", lambda c, h=h: share.at[c, h, xl, lo_half], lambda c, h=h: share.at[c, h, xl, lo_half], x_right,
            lambda c, h=h: share.at[c, h, xo, lo_half])
        add(f"xfm{h}", lambda c, h=h: share.at[c, h, xr, hi_half], lambda c, h=h: share.at[c, h, xr, hi_half], x_left,
            lambda c, h=h: share.at[c, h, xo, hi_half])
    up_slots, dn_slots = (7, 6, 4, 2), (7, 5, 3, 1)
    for which in range(2):
        block = pl.ds(which * 4, 4)
        for way in range(2):
            for step in range(0 if which == way else 1, 4):
                slot = (up_slots, dn_slots)[way][step]
                add(f"r{way}{which}{step}", lambda c, s=slot, block=block: outs.at[c, s, block],
                    lambda c, w=way, s=step, block=block: ring_in.at[c, w, s, block], (z_right, z_left)[way])
        add(f"tp{which}", lambda c, w=which: rows_out.at[c, 2, w], lambda c, w=which: rows_in.at[c, 0, w], y_right)
        add(f"tm{which}", lambda c, w=which: rows_out.at[c, 1, w], lambda c, w=which: rows_in.at[c, 1, w], y_left)
        add(f"tf{which}", lambda c, w=which: rows_out.at[c, 3, w], lambda c, w=which: rows_in.at[c, 2, w], y_far)
    assert len(copies) == send_sem.shape[1], len(copies)

    def describe(src, dst, c, index, peer):
        return pltpu.make_async_remote_copy(
            src_ref=src, dst_ref=dst, send_sem=send_sem.at[c, index], recv_sem=recv_sem.at[c, index],
            device_id=peer, device_id_type=MESH,
        )

    def start(c, *names):
        for name in names:
            index, src, dst, peer, land = copies[name]
            describe(src(c), dst(c), c, index, peer).start()

    def got(c, *names):
        for name in names:
            index, src, dst, peer, land = copies[name]
            describe(land(c), land(c), c, index, peer).wait_recv()

    def sent(c, *names):
        for name in names:
            index, src, dst, peer, land = copies[name]
            describe(src(c), dst(c), c, index, peer).wait_send()

    def mask_row(i):
        return (14 * z + i) // 4

    def load_gate_up(i):
        loads[i].wait()

        @pl.loop(0, tok_ref.shape[1] // EDGE)
        def _(f):
            at = pl.ds(pl.multiple_of(f * EDGE, EDGE), EDGE)
            turned[...] = window[i, at, :].T
            for g in range(14):
                rows = pl.ds(pl.multiple_of(lax.rem(z, 2) * 64 + g * GRAIN, GRAIN), GRAIN)
                keep = inner_ref[f, mask_row(g)].astype(F32)
                into = pl.ds(i * own + g % 7 * GRAIN, GRAIN)
                wgu[g // 7, into, at] = (turned[rows, :].astype(F32) * keep).astype(BF16)

    def load_down():
        loads[2].wait()
        loads[3].wait()

        @pl.loop(0, tok_ref.shape[1] // EDGE)
        def _(f):
            at = pl.ds(pl.multiple_of(f * EDGE, EDGE), EDGE)
            for g in range(14):
                rows = pl.ds(g % 7 * GRAIN, GRAIN)
                keep = outer_ref[f, mask_row(g)].astype(F32)
                wd[g // 7, rows, at] = (wd[g // 7, rows, at].astype(F32) * keep).astype(BF16)

    def gather(step, c):
        if step == 0:
            start(c, "zp0", "zm0", "yp0", "ym0")
        elif step == 1:
            got(c, "zp0", "zm0")
            start(c, "zp1", "zm1", "yp1", "ym1")
            got(c, "yp0", "ym0")
            start(c, "yfp0", "yfm0")
        elif step == 2:
            got(c, "zp1", "zm1")
            start(c, "zp2", "zm2", "yp2", "ym2")
        elif step == 3:
            got(c, "zp2", "zm2")
            start(c, "zp3", "zm3")
            got(c, "yp1", "ym1")
            start(c, "yfp1", "yfm1")
        elif step == 4:
            got(c, "zp3", "zm3")
            start(c, "yp3", "ym3")
            got(c, "yp2", "ym2")
            start(c, "yfp2", "yfm2")
        elif step == 5:
            got(c, "yp3", "ym3")
            start(c, "yfp3", "yfm3")
        else:
            for g in range(len(GROUPS)):
                got(c, f"yfp{g}", f"yfm{g}")

    def rows_of(c, first_y, count, which):
        return act[c, pl.ds(first_y, count), :, which].reshape(count * SLOTS * ROWS, -1)

    def project(h, c):
        @pl.loop(0, 2)
        def _(p):
            gu = dot(wgu[h], rows_of(c, 2 * p, 2, 0), (1, 1)).astype(BF16)
            part[c, h, 2 * p, pl.ds(0, unit)] = gu[:, :128]
            part[c, h, 2 * p + 1, pl.ds(0, unit)] = gu[:, 128:]
            hg = dot(wd[h], rows_of(c, 2 * p, 2, 1), (1, 1)).astype(BF16)
            part[c, h, 2 * p, pl.ds(unit, own)] = hg[:, :128]
            part[c, h, 2 * p + 1, pl.ds(unit, own)] = hg[:, 128:]

        start(c, f"xop{h}", f"xom{h}", f"xdp{h}", f"xdm{h}")

    tile = 112

    def middle_sums(h, c):
        got(c, f"xop{h}", f"xom{h}")

        @pl.loop(0, half // tile)
        def _(i):
            at = pl.ds(pl.multiple_of(i * tile, 16), tile)
            up = pl.ds(pl.multiple_of(half + i * tile, 16), tile)
            part[c, h, xr, at] = (part[c, h, xr, at].astype(F32) + opp_in[c, h, 0, at].astype(F32)).astype(BF16)
            part[c, h, xl, up] = (part[c, h, xl, up].astype(F32) + opp_in[c, h, 1, at].astype(F32)).astype(BF16)

        start(c, f"xsp{h}", f"xsm{h}")

    def gated(h, c):
        got(c, f"xdp{h}", f"xdm{h}", f"xsp{h}", f"xsm{h}")

        def total(at):
            return part[c, h, x, at].astype(F32) + sum_in[c, h, 0, at].astype(F32) + sum_in[c, h, 1, at].astype(F32)

        @pl.loop(0, own // GRAIN)
        def _(i):
            at = pl.ds(pl.multiple_of(i * GRAIN, GRAIN), GRAIN)
            at_up = pl.ds(pl.multiple_of(own + i * GRAIN, GRAIN), GRAIN)
            at_dn = pl.ds(pl.multiple_of(unit + i * GRAIN, GRAIN), GRAIN)
            gate, up, grad = total(at), total(at_up), total(at_dn)
            sig = 1.0 / (1.0 + jnp.exp(-gate))
            act_gate = gate * sig
            share[c, h, x, at_dn] = (act_gate * up).astype(BF16)
            share[c, h, x, at] = (grad * up * sig * (1.0 + gate * (1.0 - sig))).astype(BF16)
            share[c, h, x, at_up] = (grad * act_gate).astype(BF16)

        start(c, f"xap{h}", f"xam{h}")

    def forward_shares(h, c):
        got(c, f"xap{h}", f"xam{h}")
        start(c, f"xfp{h}", f"xfm{h}")

    def joined(c, h, rows, first_part, count):
        return jnp.concatenate([share[c, h, first_part + i, rows] for i in range(count)], axis=1)

    def both(c, rows, first_part, count):
        return jnp.concatenate([joined(c, h, rows, first_part, count) for h in range(2)], axis=0)

    def outputs(c):
        got(c, "xfp0", "xfm0", "xfp1", "xfm1")
        for which in range(2):

            @pl.loop(0, 2)
            def _(p):
                if which == 0:
                    left, right = both(c, pl.ds(unit, own), 2 * p, 2), wd[...].reshape(unit, -1)
                else:
                    left, right = both(c, pl.ds(0, unit), 2 * p, 2), wgu[...].reshape(2 * unit, -1)
                done = dot(left, right, (0, 0)).astype(BF16).reshape(2, SLOTS, ROWS, -1)
                outs[c, :, 4 * which + 2 * p] = done[0]
                outs[c, :, 4 * which + 2 * p + 1] = done[1]

            start(c, f"r{which}{which}0")
            start(c, f"r{1 - which}{which}1")

    def ring(which_long, step, c):
        for way in range(2):
            which = way if which_long else 1 - way
            got(c, f"r{way}{which}{step - 1}")
            slot = (up_slots, dn_slots)[way][step]

            @pl.loop(4 * which, 4 * which + 4)
            def _(i):
                outs[c, slot, i] = (outs[c, slot, i].astype(F32) + ring_in[c, way, step - 1, i].astype(F32)).astype(BF16)

            start(c, f"r{way}{which}{step}")

    def own_sum(c, i):
        return outs[c, 0, i].astype(F32) + ring_in[c, 0, 3, i].astype(F32) + ring_in[c, 1, 3, i].astype(F32)

    def leave(c):
        for which in range(2):
            got(c, f"r0{which}3", f"r1{which}3")
            for dest in range(1, 4):
                rows_out[c, dest, which] = own_sum(c, which * 4 + dest).astype(BF16)
            start(c, f"tp{which}", f"tm{which}", f"tf{which}")

    def finish_rows(c):
        at = pl.ds(pl.multiple_of(c * ROWS, ROWS), ROWS)
        for which, ref in ((0, lo_ref), (1, ig_ref)):
            got(c, f"tp{which}", f"tm{which}", f"tf{which}")
            total = own_sum(c, which * 4)
            for i in range(3):
                total = total + rows_in[c, i, which].astype(F32)
            ref[at, :] = total.astype(BF16)

    width = 256

    def weight_grads(c):
        @pl.loop(0, acc.shape[2] // width)
        def _(n):
            lanes = pl.ds(pl.multiple_of(n * width, width), width)
            tokens = act[c, :, :, 0, :, lanes].reshape(4 * SLOTS * ROWS, width)
            grads = act[c, :, :, 1, :, lanes].reshape(4 * SLOTS * ROWS, width)
            for h in range(2):
                acc[h, pl.ds(0, unit), lanes] += dot(joined(c, h, pl.ds(0, unit), 0, 4), tokens, (1, 0))
                acc[h, pl.ds(unit, own), lanes] += dot(joined(c, h, pl.ds(unit, own), 0, 4), grads, (1, 0))

    def pair_copy():
        return pltpu.make_async_remote_copy(
            src_ref=pair_out, dst_ref=pair_in, send_sem=pair_send, recv_sem=pair_recv,
            device_id=sibling, device_id_type=MESH,
        )

    def pair_start():
        pair_out[...] = acc[1 - k].astype(BF16)
        pair_copy().start()

    def pair_finish():
        pair_copy().wait_recv()

        @pl.loop(0, tok_ref.shape[1] // EDGE)
        def _(f):
            at = pl.ds(pl.multiple_of(f * EDGE, EDGE), EDGE)
            for i, ref in enumerate((gate_ref, up_ref, down_ref)):
                pieces = []
                for g in range(7):
                    rows = pl.ds(i * own + g * GRAIN, GRAIN)
                    block = mask_row(7 * k + g)
                    keep = (inner_ref if i < 2 else outer_ref)[f, block].astype(F32)
                    pieces.append((acc[k, rows, at] + pair_in[rows, at].astype(F32)) * keep)
                ref[:, at] = jnp.concatenate(pieces, axis=0).astype(BF16)

    gather(0, 0)
    acc[...] = jnp.zeros_like(acc)

    @pl.loop(0, CHUNKS + 2)
    def _(s):
        ahead, now, behind = s, s - 1, s - 2

        def when_ahead(f, *a):
            pl.when(ahead < CHUNKS)(lambda: f(*a, ahead))

        def when_now(f, *a):
            pl.when((now >= 0) & (now < CHUNKS))(lambda: f(*a, now))

        def when_behind(f, *a):
            pl.when(behind >= 0)(lambda: f(*a, behind))

        def at_end(f):
            pl.when(s == CHUNKS + 1)(f)

        def at_first(f, *a):
            pl.when(s == 0)(lambda: f(*a))

        when_ahead(gather, 1)
        at_first(load_gate_up, 0)
        when_now(middle_sums, 0)
        when_ahead(gather, 2)
        at_first(load_gate_up, 1)
        when_behind(ring, True, 1)
        when_ahead(gather, 3)
        when_now(middle_sums, 1)
        when_behind(ring, False, 2)
        when_ahead(gather, 4)
        at_first(load_down)
        when_now(gated, 0)
        when_behind(ring, True, 2)
        when_now(gated, 1)
        when_ahead(gather, 5)
        when_behind(ring, False, 3)
        when_behind(weight_grads)
        at_end(pair_start)
        when_now(forward_shares, 0)
        when_behind(ring, True, 3)
        when_now(forward_shares, 1)
        at_end(pair_finish)
        when_ahead(gather, 6)
        pl.when(s + 1 < CHUNKS)(lambda: gather(0, s + 1))
        when_ahead(project, 0)
        when_ahead(project, 1)
        when_behind(leave)
        when_now(outputs)
        when_behind(finish_rows)
        pl.when(behind >= 0)(lambda: sent(behind, *copies))

    pair_copy().wait_send()


def on_device(tokens_in, out_grad, gate_weight, up_weight, down_weight, inner_mask, outer_mask):
    features, width = gate_weight.shape
    own = width // lax.axis_size("dp")
    rows = tokens_in.shape[0]
    full = 3 * own
    vmem = pl.BlockSpec(memory_space=pltpu.VMEM)
    smem = pl.BlockSpec(memory_space=pltpu.SMEM)
    anywhere = pl.BlockSpec(memory_space=pl.ANY)
    layer_out, input_grad, gate_grad, up_grad, down_grad = pl.pallas_call(
        layer_kernel,
        name="layer",
        out_shape=(
            jax.ShapeDtypeStruct((rows, features), BF16),
            jax.ShapeDtypeStruct((rows, features), BF16),
            jax.ShapeDtypeStruct((own, features), BF16),
            jax.ShapeDtypeStruct((own, features), BF16),
            jax.ShapeDtypeStruct((own, features), BF16),
        ),
        in_specs=[vmem, vmem, anywhere, anywhere, anywhere, smem, smem],
        out_specs=(vmem,) * 5,
        scratch_shapes=[
            pltpu.VMEM((CHUNKS, 4, SLOTS, 2, ROWS, features), BF16),
            pltpu.VMEM((CHUNKS, 2, 4, full, 128), BF16),
            pltpu.VMEM((CHUNKS, 2, 2, full // 2, 128), BF16),
            pltpu.VMEM((CHUNKS, 2, 2, full, 128), BF16),
            pltpu.VMEM((CHUNKS, 2, 4, full, 128), BF16),
            pltpu.VMEM((CHUNKS, SLOTS, 8, ROWS, features), BF16),
            pltpu.VMEM((CHUNKS, 2, 4, 8, ROWS, features), BF16),
            pltpu.VMEM((CHUNKS, 4, 2, ROWS, features), BF16),
            pltpu.VMEM((CHUNKS, 3, 2, ROWS, features), BF16),
            pltpu.VMEM((2, full, features), F32),
            pltpu.VMEM((full, features), BF16),
            pltpu.VMEM((full, features), BF16),
            pltpu.VMEM((2, 2 * own, features), BF16),
            pltpu.VMEM((2, own, features), BF16),
            pltpu.VMEM((2, features, WINDOW), BF16),
            pltpu.VMEM((WINDOW, EDGE), BF16),
            pltpu.SemaphoreType.DMA((CHUNKS, COPIES)),
            pltpu.SemaphoreType.DMA((CHUNKS, COPIES)),
            pltpu.SemaphoreType.DMA,
            pltpu.SemaphoreType.DMA,
            pltpu.SemaphoreType.DMA((4,)),
        ],
        compiler_params=pltpu.CompilerParams(
            collective_id=0, has_side_effects=True, vmem_limit_bytes=58 * 2**20
        ),
    )(tokens_in, out_grad, gate_weight, up_weight, down_weight, inner_mask, outer_mask.T)
    return (layer_out, input_grad, gate_grad.T, up_grad.T, down_grad)


def solution(mesh):
    placed = (
        P(("col", "dp"), "row"),
        P(("col", "dp"), "row"),
        P("row", "col"),
        P("row", "col"),
        P("col", "row"),
        P("row", "col"),
        P("col", "row"),
    )
    return jax.shard_map(
        on_device,
        mesh=mesh,
        in_specs=placed,
        out_specs=(
            P(("col", "dp"), "row"),
            P(("col", "dp"), "row"),
            P("row", ("col", "dp")),
            P("row", ("col", "dp")),
            P(("col", "dp"), "row"),
        ),
        check_vma=False,
    )
```

time: 199 us -> 159 us (0.80)
  Pallas kernels: 165 us -> 149 us
  local copies, waits for them, and re-layouts: 24 us -> 8.52 us
  other arithmetic: 6.73 us -> 0 us
    pallas_call x1, Pallas kernels: 165 us -> 149 us  [on_device(): pl.pallas_call(layer_kernel, name='layer', out_shape=(jax.ShapeDtypeStruc...]
    unnamed x13 -> x5, local copies, waits for them, and re-layouts: 15.7 us -> 8.52 us
    mul x2 -> x0, other arithmetic: 4.07 us -> none  [the longest x1 3.98 us: on_device(): lax.dynamic_slice_in_dim(gate_weight, offset, unit, 1).T * inner_slice]
    dynamic_slice x2 -> x0, local copies, waits for them, and re-layouts: 3.9 us -> none  [the longest x1 2.11 us: on_device(): lax.dynamic_slice_in_dim(up_weight, offset, unit, 1).T * inner_slice]
    concatenate x1 -> x0, other arithmetic: 2.65 us -> none  [on_device(): joined = jnp.concatenate([gate_eff, up_eff], axis=0)]
    transpose x1 -> x0, local copies, waits for them, and re-layouts: 2.14 us -> none  [on_device(): return (layer_out, input_grad, gate_up[0].T, gate_up[1].T, down_grad)]
    broadcast_in_dim x2 -> x0, local copies, waits for them, and re-layouts: 2.03 us -> none  [expand_blocks(): jnp.broadcast_to(scaled[:, None, :, None], (count_rows, edge, count_cols,...]
where the time goes in v3:
time: 159 us
  Pallas kernels  149 us (94%)
  local copies, waits for them, and re-layouts  8.52 us (5%)
    pallas_call x1, Pallas kernels, on_device(): pl.pallas_call(layer_kernel, name='layer', out_shape=(jax.ShapeDtypeStruc...  149 us
    unnamed x5, local copies, waits for them, and re-layouts  8.52 us

profile of v3, /device:TPU:2, one launch (start us, length us, event | category | flops | bytes accessed | tf_op | source)
XLA Modules:
  0.0 158.5 jit_solution(13531467017885518284)
XLA Ops:
  0.6 149.4 %layer.1 = (bf16[48,1024]{1,0:T(8,128)(2,1)}, bf16[48,1024]{1,0:T(8,128)(2,1)}, bf16[224,1024]{1,0:T(8,128)(2,1)}, bf16[224,1024]{1,0:T(8,128)(2,1)}, bf16[224,1024]{1,0:T(8,128)(2,1)}) custom-call(bf16[48,1024]{1,0:T(8,128)(2,1)} %tok_ref.1, bf16[48,1024]{1,0:T(8,128)(2,1)} %grad_ref.1, bf16[1024,3584]{1,0:T(8,128)(2,1)} %gate_hbm.1, ...), custom_call_target="tpu_custom_call" | custom-call | tf_op jit(solution)/shard_map/layer/pallas_call | solution.py:402
  150.0 1.5 copy.17
  151.6 1.5 copy.18
  153.1 1.8 %copy.19 = bf16[1024,224]{0,1:T(8,128)(2,1)} copy(bf16[1024,224]{0,1:T(8,128)(2,1)} %bitcast.4) | data formatting | bytes 917504
  154.9 1.8 %copy.20 = bf16[1024,224]{0,1:T(8,128)(2,1)} copy(bf16[1024,224]{0,1:T(8,128)(2,1)} %bitcast.3) | data formatting | bytes 917504
  156.7 1.8 %copy.21 = bf16[224,1024]{1,0:T(8,128)(2,1)} copy(bf16[224,1024]{1,0:T(8,128)(2,1)} %get-tuple-element.24) | data formatting | bytes 917504

commit v4 on v3

--- a/solution.py
+++ b/solution.py
@@ -15,7 +15,8 @@
 GRAIN = 32
 WINDOW = 512
 GROUPS = ((0, 1), (1, 3), (3, 5), (5, 8))
-COPIES = 64
+SUM_GROUPS = ((7, 8), (5, 7), (3, 5), (0, 3))
+COPIES = 92
 
 
 def dot(left, right, dims):
@@ -25,7 +26,7 @@
 def layer_kernel(
     tok_ref, grad_ref, gate_hbm, up_hbm, down_hbm, inner_ref, outer_ref,
     lo_ref, ig_ref, gate_ref, up_ref, down_ref,
-    act, part, opp_in, sum_in, share, outs, ring_in, rows_out, rows_in, acc, pair_out, pair_in,
+    act, gact, part, opp_in, sum_in, share, outs, gouts, ring_in, gring_in, col_in, rows_out, rows_in, acc, pair_out, pair_in,
     wgu, wd, window, turned,
     send_sem, recv_sem, pair_send, pair_recv, load_sem,
 ):
@@ -64,8 +65,8 @@
     for peer in peers:
         pl.semaphore_signal(barrier, inc=1, device_id=peer, device_id_type=MESH)
     for c in range(CHUNKS):
-        act[c, 0, 0, 0] = tok_ref[pl.ds(c * ROWS, ROWS), :]
-        act[c, 0, 0, 1] = grad_ref[pl.ds(c * ROWS, ROWS), :]
+        act[c, 0, 0] = tok_ref[pl.ds(c * ROWS, ROWS), :]
+        gact[c, 0, 0] = grad_ref[pl.ds(c * ROWS, ROWS), :]
     pl.semaphore_wait(barrier, len(peers))
 
     copies = {}
@@ -73,19 +74,25 @@
     def add(name, src, dst, peer, land=None):
         copies[name] = (len(copies), src, dst, peer, dst if land is None else land)
 
-    for step in range(3):
-        up_from, up_to = (0, 1, 3)[step], (1, 3, 5)[step]
-        dn_from, dn_to = (0, 2, 4)[step], (2, 4, 6)[step]
-        add(f"zp{step}", lambda c, a=up_from: act.at[c, 0, a], lambda c, a=up_to: act.at[c, 0, a], z_right)
-        add(f"zm{step}", lambda c, a=dn_from: act.at[c, 0, a], lambda c, a=dn_to: act.at[c, 0, a], z_left)
-    add("zp3", lambda c: act.at[c, 0, 5, 0], lambda c: act.at[c, 0, 7, 0], z_right)
-    add("zm3", lambda c: act.at[c, 0, 6, 1], lambda c: act.at[c, 0, 7, 1], z_left)
+    hops = (("p", (0, 1, 3, 5), (1, 3, 5, 7), z_right), ("m", (0, 2, 4, 6), (2, 4, 6, 7), z_left))
+    for way, (letter, sources, targets, peer) in enumerate(hops):
+        for step in range(4 if way == 0 else 3):
+            add(f"z{letter}{step}", lambda c, a=sources[step]: act.at[c, 0, a], lambda c, a=targets[step]: act.at[c, 0, a], peer)
+        for j in range(2):
+            pair = pl.ds(2 * j, 2)
+            for step in range(4 if way == j else 3):
+                add(f"g{letter}{j}{step}", lambda c, a=sources[step], pair=pair: gact.at[c, a, pair],
+                    lambda c, a=targets[step], pair=pair: gact.at[c, a, pair], peer)
     for g, (a, b) in enumerate(GROUPS):
         sl = pl.ds(a, b - a)
         add(f"yp{g}", lambda c, sl=sl: act.at[c, 0, sl], lambda c, sl=sl: act.at[c, 1, sl], y_right)
         add(f"ym{g}", lambda c, sl=sl: act.at[c, 0, sl], lambda c, sl=sl: act.at[c, 2, sl], y_left)
-        add(f"yfp{g}", lambda c, sl=sl: act.at[c, 1, sl, 0], lambda c, sl=sl: act.at[c, 3, sl, 0], y_right)
-        add(f"yfm{g}", lambda c, sl=sl: act.at[c, 2, sl, 1], lambda c, sl=sl: act.at[c, 3, sl, 1], y_left)
+        if g in (0, 3):
+            add(f"yf{g}", lambda c, sl=sl: act.at[c, 1, sl], lambda c, sl=sl: act.at[c, 3, sl], y_right)
+        else:
+            add(f"yf{g}", lambda c, sl=sl: act.at[c, 2, sl], lambda c, sl=sl: act.at[c, 3, sl], y_left)
+    for i, peer in ((1, y_right), (2, y_left), (3, y_far)):
+        add(f"gy{i}", lambda c: gact.at[c, 0, 0], lambda c, i=i: gact.at[c, 0, i], peer)
     for h in range(2):
         add(f"xop{h}", lambda c, h=h: part.at[c, h, xo, lo_half], lambda c, h=h: opp_in.at[c, h, 0], x_right)
         add(f"xom{h}", lambda c, h=h: part.at[c, h, xo, hi_half], lambda c, h=h: opp_in.at[c, h, 1], x_left)
@@ -101,17 +108,23 @@
             lambda c, h=h: share.at[c, h, xo, lo_half])
         add(f"xfm{h}", lambda c, h=h: share.at[c, h, xr, hi_half], lambda c, h=h: share.at[c, h, xr, hi_half], x_left,
             lambda c, h=h: share.at[c, h, xo, hi_half])
-    up_slots, dn_slots = (7, 6, 4, 2), (7, 5, 3, 1)
-    for which in range(2):
-        block = pl.ds(which * 4, 4)
+    slots = ((7, 6, 4, 2), (7, 5, 3, 1))
+    for j in range(2):
+        pair = pl.ds(2 * j, 2)
         for way in range(2):
-            for step in range(0 if which == way else 1, 4):
-                slot = (up_slots, dn_slots)[way][step]
-                add(f"r{way}{which}{step}", lambda c, s=slot, block=block: outs.at[c, s, block],
-                    lambda c, w=way, s=step, block=block: ring_in.at[c, w, s, block], (z_right, z_left)[way])
-        add(f"tp{which}", lambda c, w=which: rows_out.at[c, 2, w], lambda c, w=which: rows_in.at[c, 0, w], y_right)
-        add(f"tm{which}", lambda c, w=which: rows_out.at[c, 1, w], lambda c, w=which: rows_in.at[c, 1, w], y_left)
-        add(f"tf{which}", lambda c, w=which: rows_out.at[c, 3, w], lambda c, w=which: rows_in.at[c, 2, w], y_far)
+            for step in range(0 if j == way else 1, 4):
+                add(f"r{j}{way}{step}", lambda c, s=slots[way][step], pair=pair: outs.at[c, s, pair],
+                    lambda c, w=way, s=step, pair=pair: ring_in.at[c, w, s, pair], (z_right, z_left)[way])
+    for i, (name, place, peer) in enumerate((("tp", 2, y_right), ("tm", 1, y_left), ("tf", 3, y_far))):
+        add(name, lambda c, a=place: rows_out.at[c, a], lambda c, i=i: rows_in.at[c, i], peer)
+    for g, (a, b) in enumerate(SUM_GROUPS):
+        sl = pl.ds(a, b - a)
+        for i, (place, peer) in enumerate(((1, y_left), (2, y_right), (3, y_far))):
+            add(f"c{g}{i}", lambda c, a=place, sl=sl: gouts.at[c, a, sl], lambda c, i=i, sl=sl: col_in.at[c, i, sl], peer)
+    for way in range(2):
+        for step in range(1 - way, 4):
+            add(f"q{way}{step}", lambda c, s=slots[way][step]: gouts.at[c, 0, s],
+                lambda c, w=way, s=step: gring_in.at[c, w, s], (z_right, z_left)[way])
     assert len(copies) == send_sem.shape[1], len(copies)
 
     def describe(src, dst, c, index, peer):
@@ -165,42 +178,61 @@
 
     def gather(step, c):
         if step == 0:
-            start(c, "zp0", "zm0", "yp0", "ym0")
+            start(c, "gy1", "gy2", "gy3", "zp0", "zm0", "yp0", "ym0")
         elif step == 1:
+            got(c, "gy1")
+            start(c, "gp00", "gm00")
+            got(c, "gy2", "gy3")
+            start(c, "gp10", "gm10")
             got(c, "zp0", "zm0")
             start(c, "zp1", "zm1", "yp1", "ym1")
             got(c, "yp0", "ym0")
-            start(c, "yfp0", "yfm0")
+            start(c, "yf0")
         elif step == 2:
             got(c, "zp1", "zm1")
             start(c, "zp2", "zm2", "yp2", "ym2")
+            for j in range(2):
+                got(c, f"gp{j}0", f"gm{j}0")
+                start(c, f"gp{j}1", f"gm{j}1")
         elif step == 3:
             got(c, "zp2", "zm2")
-            start(c, "zp3", "zm3")
+            start(c, "zp3")
             got(c, "yp1", "ym1")
-            start(c, "yfp1", "yfm1")
+            start(c, "yf1")
+            for j in range(2):
+                got(c, f"gp{j}1", f"gm{j}1")
+                start(c, f"gp{j}2", f"gm{j}2")
         elif step == 4:
-            got(c, "zp3", "zm3")
+            got(c, "zp3")
             start(c, "yp3", "ym3")
             got(c, "yp2", "ym2")
-            start(c, "yfp2", "yfm2")
+            start(c, "yf2")
+            got(c, "gp02", "gm02")
+            start(c, "gp03")
+            got(c, "gp12", "gm12")
+            start(c, "gm13")
         elif step == 5:
             got(c, "yp3", "ym3")
-            start(c, "yfp3", "yfm3")
+            start(c, "yf3")
         else:
             for g in range(len(GROUPS)):
-                got(c, f"yfp{g}", f"yfm{g}")
-
-    def rows_of(c, first_y, count, which):
-        return act[c, pl.ds(first_y, count), :, which].reshape(count * SLOTS * ROWS, -1)
+                got(c, f"yf{g}")
+            got(c, "gp03", "gm13")
+
+    def grad_rows(c, first_y, count, lanes):
+        return jnp.concatenate(
+            [gact[c, :, first_y + i, :, lanes].reshape(SLOTS * ROWS, -1) for i in range(count)], axis=0
+        )
 
     def project(h, c):
+        every = pl.ds(0, act.shape[-1])
+
         @pl.loop(0, 2)
         def _(p):
-            gu = dot(wgu[h], rows_of(c, 2 * p, 2, 0), (1, 1)).astype(BF16)
+            gu = dot(wgu[h], act[c, pl.ds(2 * p, 2)].reshape(2 * SLOTS * ROWS, -1), (1, 1)).astype(BF16)
             part[c, h, 2 * p, pl.ds(0, unit)] = gu[:, :128]
             part[c, h, 2 * p + 1, pl.ds(0, unit)] = gu[:, 128:]
-            hg = dot(wd[h], rows_of(c, 2 * p, 2, 1), (1, 1)).astype(BF16)
+            hg = dot(wd[h], grad_rows(c, 2 * p, 2, every), (1, 1)).astype(BF16)
             part[c, h, 2 * p, pl.ds(unit, own)] = hg[:, :128]
             part[c, h, 2 * p + 1, pl.ds(unit, own)] = hg[:, 128:]
 
@@ -252,51 +284,78 @@
 
     def outputs(c):
         got(c, "xfp0", "xfm0", "xfp1", "xfm1")
-        for which in range(2):
-
-            @pl.loop(0, 2)
-            def _(p):
-                if which == 0:
-                    left, right = both(c, pl.ds(unit, own), 2 * p, 2), wd[...].reshape(unit, -1)
-                else:
-                    left, right = both(c, pl.ds(0, unit), 2 * p, 2), wgu[...].reshape(2 * unit, -1)
-                done = dot(left, right, (0, 0)).astype(BF16).reshape(2, SLOTS, ROWS, -1)
-                outs[c, :, 4 * which + 2 * p] = done[0]
-                outs[c, :, 4 * which + 2 * p + 1] = done[1]
-
-            start(c, f"r{which}{which}0")
-            start(c, f"r{1 - which}{which}1")
-
-    def ring(which_long, step, c):
+
+        @pl.loop(0, 2)
+        def _(p):
+            left = both(c, pl.ds(unit, own), 2 * p, 2)
+            done = dot(left, wd[...].reshape(unit, -1), (0, 0)).astype(BF16).reshape(2, SLOTS, ROWS, -1)
+            outs[c, :, 2 * p] = done[0]
+            outs[c, :, 2 * p + 1] = done[1]
+
+        start(c, "r000", "r110", "r011", "r101")
+
+        @pl.loop(0, 2)
+        def _(p):
+            left = both(c, pl.ds(0, unit), 2 * p, 2)
+            done = dot(left, wgu[...].reshape(2 * unit, -1), (0, 0)).astype(BF16).reshape(2, SLOTS, ROWS, -1)
+            gouts[c, 2 * p] = done[0]
+            gouts[c, 2 * p + 1] = done[1]
+
+        for g in range(len(SUM_GROUPS)):
+            start(c, f"c{g}0", f"c{g}1", f"c{g}2")
+
+    def ring(step, c):
+        for j, way, n in ((0, 0, step), (1, 1, step), (0, 1, step + 1), (1, 0, step + 1)):
+            if n > 3:
+                continue
+            got(c, f"r{j}{way}{n - 1}")
+            slot = slots[way][n]
+            for i in (2 * j, 2 * j + 1):
+                outs[c, slot, i] = (outs[c, slot, i].astype(F32) + ring_in[c, way, n - 1, i].astype(F32)).astype(BF16)
+            start(c, f"r{j}{way}{n}")
+
+    def column(step, c):
+        got(c, f"c{step}0", f"c{step}1", f"c{step}2")
+        first, end = SUM_GROUPS[step]
+        arriving = {}
         for way in range(2):
-            which = way if which_long else 1 - way
-            got(c, f"r{way}{which}{step - 1}")
-            slot = (up_slots, dn_slots)[way][step]
-
-            @pl.loop(4 * which, 4 * which + 4)
-            def _(i):
-                outs[c, slot, i] = (outs[c, slot, i].astype(F32) + ring_in[c, way, step - 1, i].astype(F32)).astype(BF16)
-
-            start(c, f"r{way}{which}{step}")
+            if step > 1 - way:
+                arriving[slots[way][step]] = way
+        for slot in range(end - 1, first - 1, -1):
+            total = gouts[c, 0, slot].astype(F32)
+            for i in range(3):
+                total = total + col_in[c, i, slot].astype(F32)
+            if slot in arriving:
+                way = arriving[slot]
+                got(c, f"q{way}{step - 1}")
+                total = total + gring_in[c, way, step - 1].astype(F32)
+            gouts[c, 0, slot] = total.astype(BF16)
+        for way in range(2):
+            if step >= 1 - way:
+                start(c, f"q{way}{step}")
+
+    def finish_column(c):
+        got(c, "q03", "q13")
+        at = pl.ds(pl.multiple_of(c * ROWS, ROWS), ROWS)
+        total = gouts[c, 0, 0].astype(F32) + gring_in[c, 0, 3].astype(F32) + gring_in[c, 1, 3].astype(F32)
+        ig_ref[at, :] = total.astype(BF16)
 
     def own_sum(c, i):
         return outs[c, 0, i].astype(F32) + ring_in[c, 0, 3, i].astype(F32) + ring_in[c, 1, 3, i].astype(F32)
 
     def leave(c):
-        for which in range(2):
-            got(c, f"r0{which}3", f"r1{which}3")
-            for dest in range(1, 4):
-                rows_out[c, dest, which] = own_sum(c, which * 4 + dest).astype(BF16)
-            start(c, f"tp{which}", f"tm{which}", f"tf{which}")
+        got(c, "r003", "r013", "r103", "r113")
+        for dest, name in ((3, "tf"), (2, "tp"), (1, "tm")):
+            rows_out[c, dest] = own_sum(c, dest).astype(BF16)
+            start(c, name)
 
     def finish_rows(c):
         at = pl.ds(pl.multiple_of(c * ROWS, ROWS), ROWS)
-        for which, ref in ((0, lo_ref), (1, ig_ref)):
-            got(c, f"tp{which}", f"tm{which}", f"tf{which}")
-            total = own_sum(c, which * 4)
-            for i in range(3):
-                total = total + rows_in[c, i, which].astype(F32)
-            ref[at, :] = total.astype(BF16)
+        got(c, "tp", "tm", "tf")
+        total = own_sum(c, 0)
+        for i in range(3):
+            total = total + rows_in[c, i].astype(F32)
+        lo_ref[at, :] = total.astype(BF16)
 
     width = 256
 
@@ -304,8 +363,8 @@
         @pl.loop(0, acc.shape[2] // width)
         def _(n):
             lanes = pl.ds(pl.multiple_of(n * width, width), width)
-            tokens = act[c, :, :, 0, :, lanes].reshape(4 * SLOTS * ROWS, width)
-            grads = act[c, :, :, 1, :, lanes].reshape(4 * SLOTS * ROWS, width)
+            tokens = act[c, :, :, :, lanes].reshape(4 * SLOTS * ROWS, width)
+            grads = grad_rows(c, 0, 4, lanes)
             for h in range(2):
                 acc[h, pl.ds(0, unit), lanes] += dot(joined(c, h, pl.ds(0, unit), 0, 4), tokens, (1, 0))
                 acc[h, pl.ds(unit, own), lanes] += dot(joined(c, h, pl.ds(unit, own), 0, 4), grads, (1, 0))
@@ -336,6 +395,12 @@
                 ref[:, at] = jnp.concatenate(pieces, axis=0).astype(BF16)
 
     gather(0, 0)
+    load_gate_up(0)
+    gather(1, 0)
+    load_gate_up(1)
+    gather(2, 0)
+    load_down()
+    gather(3, 0)
     acc[...] = jnp.zeros_like(acc)
 
     @pl.loop(0, CHUNKS + 2)
@@ -354,37 +419,37 @@
         def at_end(f):
             pl.when(s == CHUNKS + 1)(f)
 
-        def at_first(f, *a):
-            pl.when(s == 0)(lambda: f(*a))
-
-        when_ahead(gather, 1)
-        at_first(load_gate_up, 0)
+        def when_next(f, *a):
+            pl.when(s + 1 < CHUNKS)(lambda: f(*a, s + 1))
+
         when_now(middle_sums, 0)
-        when_ahead(gather, 2)
-        at_first(load_gate_up, 1)
-        when_behind(ring, True, 1)
-        when_ahead(gather, 3)
+        when_ahead(gather, 4)
+        when_behind(ring, 1)
         when_now(middle_sums, 1)
-        when_behind(ring, False, 2)
-        when_ahead(gather, 4)
-        at_first(load_down)
+        when_behind(column, 0)
         when_now(gated, 0)
-        when_behind(ring, True, 2)
+        when_ahead(gather, 5)
+        when_behind(ring, 2)
         when_now(gated, 1)
-        when_ahead(gather, 5)
-        when_behind(ring, False, 3)
+        when_behind(column, 1)
+        when_next(gather, 0)
+        when_ahead(gather, 6)
+        when_behind(ring, 3)
         when_behind(weight_grads)
         at_end(pair_start)
         when_now(forward_shares, 0)
-        when_behind(ring, True, 3)
+        when_next(gather, 1)
+        when_behind(column, 2)
+        when_ahead(project, 0)
         when_now(forward_shares, 1)
+        when_ahead(project, 1)
+        when_next(gather, 2)
+        when_behind(leave)
+        when_behind(column, 3)
+        when_now(outputs)
+        when_next(gather, 3)
         at_end(pair_finish)
-        when_ahead(gather, 6)
-        pl.when(s + 1 < CHUNKS)(lambda: gather(0, s + 1))
-        when_ahead(project, 0)
-        when_ahead(project, 1)
-        when_behind(leave)
-        when_now(outputs)
+        when_behind(finish_column)
         when_behind(finish_rows)
         pl.when(behind >= 0)(lambda: sent(behind, *copies))
 
@@ -412,15 +477,19 @@
         in_specs=[vmem, vmem, anywhere, anywhere, anywhere, smem, smem],
         out_specs=(vmem,) * 5,
         scratch_shapes=[
-            pltpu.VMEM((CHUNKS, 4, SLOTS, 2, ROWS, features), BF16),
+            pltpu.VMEM((CHUNKS, 4, SLOTS, ROWS, features), BF16),
+            pltpu.VMEM((CHUNKS, SLOTS, 4, ROWS, features), BF16),
             pltpu.VMEM((CHUNKS, 2, 4, full, 128), BF16),
             pltpu.VMEM((CHUNKS, 2, 2, full // 2, 128), BF16),
             pltpu.VMEM((CHUNKS, 2, 2, full, 128), BF16),
             pltpu.VMEM((CHUNKS, 2, 4, full, 128), BF16),
-            pltpu.VMEM((CHUNKS, SLOTS, 8, ROWS, features), BF16),
-            pltpu.VMEM((CHUNKS, 2, 4, 8, ROWS, features), BF16),
-            pltpu.VMEM((CHUNKS, 4, 2, ROWS, features), BF16),
-            pltpu.VMEM((CHUNKS, 3, 2, ROWS, features), BF16),
+            pltpu.VMEM((CHUNKS, SLOTS, 4, ROWS, features), BF16),
+            pltpu.VMEM((CHUNKS, 4, SLOTS, ROWS, features), BF16),
+            pltpu.VMEM((CHUNKS, 2, 4, 4, ROWS, features), BF16),
+            pltpu.VMEM((CHUNKS, 2, 4, ROWS, features), BF16),
+            pltpu.VMEM((CHUNKS, 3, SLOTS, ROWS, features), BF16),
+            pltpu.VMEM((CHUNKS, 4, ROWS, features), BF16),
+            pltpu.VMEM((CHUNKS, 3, ROWS, features), BF16),
             pltpu.VMEM((2, full, features), F32),
             pltpu.VMEM((full, features), BF16),
             pltpu.VMEM((full, features), BF16),

time: 159 us -> 153 us (0.962)
  Pallas kernels: 149 us -> 143 us
    pallas_call x1, Pallas kernels: 149 us -> 143 us  [on_device(): pl.pallas_call(layer_kernel, name='layer', out_shape=(jax.ShapeDtypeStruc...]
where the time goes in v4:
time: 153 us; the launch traced here: 152 us
  Pallas kernels  143 us (93%)
  local copies, waits for them, and re-layouts  8.52 us (6%)
    pallas_call x1, Pallas kernels, on_device(): pl.pallas_call(layer_kernel, name='layer', out_shape=(jax.ShapeDtypeStruc...  143 us
    unnamed x5, local copies, waits for them, and re-layouts  8.52 us

profile of v4, /device:TPU:2, one launch (start us, length us, event | category | flops | bytes accessed | tf_op | source)
XLA Modules:
  0.0 152.1 jit_solution(11969567778794336349)
XLA Ops:
  0.6 142.9 %layer.1 = (bf16[48,1024]{1,0:T(8,128)(2,1)}, bf16[48,1024]{1,0:T(8,128)(2,1)}, bf16[224,1024]{1,0:T(8,128)(2,1)}, bf16[224,1024]{1,0:T(8,128)(2,1)}, bf16[224,1024]{1,0:T(8,128)(2,1)}) custom-call(bf16[48,1024]{1,0:T(8,128)(2,1)} %tok_ref.1, bf16[48,1024]{1,0:T(8,128)(2,1)} %grad_ref.1, bf16[1024,3584]{1,0:T(8,128)(2,1)} %gate_hbm.1, ...), custom_call_target="tpu_custom_call" | custom-call | tf_op jit(solution)/shard_map/layer/pallas_call | solution.py:467
  143.6 1.5 %copy.17 = bf16[48,1024]{1,0:T(8,128)(2,1)} copy(bf16[48,1024]{1,0:T(8,128)(2,1)} %get-tuple-element.20) | data formatting | bytes 196608
  145.1 1.5 %copy.18 = bf16[48,1024]{1,0:T(8,128)(2,1)} copy(bf16[48,1024]{1,0:T(8,128)(2,1)} %get-tuple-element.21) | data formatting | bytes 196608
  146.7 1.8 %copy.19 = bf16[1024,224]{0,1:T(8,128)(2,1)} copy(bf16[1024,224]{0,1:T(8,128)(2,1)} %bitcast.4) | data formatting | bytes 917504
  148.5 1.8 %copy.20 = bf16[1024,224]{0,1:T(8,128)(2,1)} copy(bf16[1024,224]{0,1:T(8,128)(2,1)} %bitcast.3) | data formatting | bytes 917504
  150.3 1.8 %copy.21 = bf16[224,1024]{1,0:T(8,128)(2,1)} copy(bf16[224,1024]{1,0:T(8,128)(2,1)} %get-tuple-element.24) | data formatting | bytes 917504

commit v5 on v4

--- a/solution.py
+++ b/solution.py
@@ -440,8 +440,8 @@
         when_now(forward_shares, 0)
         when_next(gather, 1)
         when_behind(column, 2)
+        when_now(forward_shares, 1)
         when_ahead(project, 0)
-        when_now(forward_shares, 1)
         when_ahead(project, 1)
         when_next(gather, 2)
         when_behind(leave)

time: 153 us -> 150 us (0.980)
  Pallas kernels: 143 us -> 140 us
    pallas_call x1, Pallas kernels: 143 us -> 140 us  [on_device(): pl.pallas_call(layer_kernel, name='layer', out_shape=(jax.ShapeDtypeStruc...]
where the time goes in v5:
time: 150 us; the launch traced here: 149 us
  Pallas kernels  140 us (93%)
  local copies, waits for them, and re-layouts  8.52 us (6%)
    pallas_call x1, Pallas kernels, on_device(): pl.pallas_call(layer_kernel, name='layer', out_shape=(jax.ShapeDtypeStruc...  140 us
    unnamed x5, local copies, waits for them, and re-layouts  8.52 us

profile of v5, /device:TPU:2, one launch (start us, length us, event | category | flops | bytes accessed | tf_op | source)
XLA Modules:
  0.0 149.4 jit_solution(10726991456390900140)
XLA Ops:
  0.6 140.2 %layer.1 = (bf16[48,1024]{1,0:T(8,128)(2,1)}, bf16[48,1024]{1,0:T(8,128)(2,1)}, bf16[224,1024]{1,0:T(8,128)(2,1)}, bf16[224,1024]{1,0:T(8,128)(2,1)}, bf16[224,1024]{1,0:T(8,128)(2,1)}) custom-call(bf16[48,1024]{1,0:T(8,128)(2,1)} %tok_ref.1, bf16[48,1024]{1,0:T(8,128)(2,1)} %grad_ref.1, bf16[1024,3584]{1,0:T(8,128)(2,1)} %gate_hbm.1, ...), custom_call_target="tpu_custom_call" | custom-call | tf_op jit(solution)/shard_map/layer/pallas_call | solution.py:467
  140.8 1.5 %copy.17 = bf16[48,1024]{1,0:T(8,128)(2,1)} copy(bf16[48,1024]{1,0:T(8,128)(2,1)} %get-tuple-element.20) | data formatting | bytes 196608
  142.4 1.5 %copy.18 = bf16[48,1024]{1,0:T(8,128)(2,1)} copy(bf16[48,1024]{1,0:T(8,128)(2,1)} %get-tuple-element.21) | data formatting | bytes 196608
  143.9 1.8 %copy.19 = bf16[1024,224]{0,1:T(8,128)(2,1)} copy(bf16[1024,224]{0,1:T(8,128)(2,1)} %bitcast.4) | data formatting | bytes 917504
  145.7 1.8 %copy.20 = bf16[1024,224]{0,1:T(8,128)(2,1)} copy(bf16[1024,224]{0,1:T(8,128)(2,1)} %bitcast.3) | data formatting | bytes 917504
  147.6 1.8 %copy.21 = bf16[224,1024]{1,0:T(8,128)(2,1)} copy(bf16[224,1024]{1,0:T(8,128)(2,1)} %get-tuple-element.24) | data formatting | bytes 917504
